TPU v7x, 32 devices: a whole 2x2x4 slice. The times are simulated.
32 devices in a mesh: trial: 2 (over core), tmpl: 16 (over z, y, x).
Axes of the slice: x: 2, y: 2, z: 4, core: 2. Of those that a mesh axis runs over, the one named last changes fastest.
Arguments:
- spectra: bfloat16 [2, 2, 16, 2, 16896], P(None, 'trial', 'tmpl'), may hold values from -6 to 6
- half_spectra: bfloat16 [2, 2, 16, 2, 8704], P(None, 'trial', 'tmpl'), may hold values from -6 to 6
- kernels: bfloat16 [256, 2, 512], P('tmpl'), may hold values from -0.1875 to 0.1875
- owners: int32 [2, 2], replicated, may hold values from 0 to 31, as said below
- counts: int32 [16], replicated, may hold values from 12 to 16, as said below
- partners: int32 [256], replicated, may hold values from -1 to 255, as said below
Outputs:
- powers: bfloat16 [2, 2, 256, 16384], P(None, 'trial', 'tmpl')
Inputs may be any that keep to these rules, and one draw needn't show every extreme that they name: owners[w, t] = i * 16 + c names the device with trial index i and tmpl index c that holds window w's data of trial t; the two trials of a window lie on different trial indices, and the trial index holding trial 0 alternates from one window to the next; in some window the two trials lie on devices 0 and 31. The live templates of tmpl index d are its first counts[d]; some index has all 16 live. For a live template j, partners[j] is a live template; the live templates of one tmpl index name templates of any one tmpl index at most 1 times, and some index does so exactly 1 times; partners[j] = -1 for every template that is not live.
All inputs are finite; a program needn't handle non-finite values.
Results may differ from a plain program's by a relative error of at most 0.004.
Values may be sent and summed in bfloat16 or wider, within the bound.
A program may use at most 128 MiB of HBM per device.

v0:
```python
import jax
import jax.numpy as jnp
from jax import lax
from jax.sharding import PartitionSpec as P


def spread(block, axis, source):
    block = jnp.where(lax.axis_index(axis) == source, block, jnp.zeros_like(block))
    return lax.psum(block, axis)


def swapped(x, axis, bit):
    return lax.ppermute(x, axis, [(i, i ^ 1 << bit) for i in range(lax.axis_size(axis))])


def hankel_rows(signal, tap_count, columns):
    length = signal.shape[1]
    repeated = jnp.broadcast_to(signal[:, None, :], (2, tap_count + 1, length)).reshape(
        2, (tap_count + 1) * length
    )
    skewed = repeated[:, : tap_count * (length + 1)].reshape(2, tap_count, length + 1)
    return skewed[:, :, :columns].reshape(2 * tap_count, columns)


def kernel_matrix(kernel_set):
    real_part = kernel_set[:, 0, :]
    imag_part = kernel_set[:, 1, :]
    upper_rows = jnp.concatenate([real_part, -imag_part], axis=1)
    lower_rows = jnp.concatenate([imag_part, real_part], axis=1)
    return jnp.concatenate([upper_rows, lower_rows], axis=0)


def power_rows(weights, stacked):
    product = jnp.dot(weights, stacked, preferred_element_type=jnp.float32)
    middle = weights.shape[0] // 2
    return product[:middle] * product[:middle] + product[middle:] * product[middle:]


def blocked_powers(weights, signal, tap_count, columns):
    block_rows = min(columns, 1024)

    def add_block(number, result):
        first_bin = number * block_rows
        segment = lax.dynamic_slice_in_dim(signal, first_bin, block_rows + tap_count, 1)
        values = power_rows(weights, hankel_rows(segment, tap_count, block_rows))
        return lax.dynamic_update_slice_in_dim(result, values, first_bin, 1)

    initial = jnp.zeros((weights.shape[0] // 2, columns), jnp.float32)
    return lax.fori_loop(0, columns // block_rows, add_block, initial)


def read_plan(partners, counts, per_device, width):
    pair_table = partners.reshape(width, per_device)
    positions = jnp.arange(per_device, dtype=jnp.int32)
    live_mask = positions[None, :] < counts[:, None]
    source = jnp.where(live_mask, pair_table // per_device, -1)
    holder_slot = pair_table % per_device
    earlier = positions[:, None] > positions[None, :]
    matches = (source[:, :, None] == source[:, None, :]) & earlier[None, :, :]
    ranking = jnp.sum(matches.astype(jnp.int32), axis=2)
    return (live_mask, source, holder_slot, ranking)


def body(spectra, half_spectra, kernels, owners, counts, partners):
    width = lax.axis_size("tmpl")
    device = lax.axis_index("tmpl")
    trial_index = lax.axis_index("trial")
    per_device = kernels.shape[0]
    tap_count = kernels.shape[2]
    windows = spectra.shape[0]
    bins_whole = spectra.shape[4] - tap_count
    bins_half = half_spectra.shape[4] - tap_count
    capacity = max(1, per_device // width)
    weights = kernel_matrix(kernels)
    stored = jnp.concatenate([spectra[:, 0, 0], half_spectra[:, 0, 0]], axis=2)
    slabs = []
    for window in range(windows):
        row_owner = owners[window] // width
        held_trial = jnp.where(row_owner[0] == trial_index, 0, 1)
        column = owners[window][held_trial] % width
        arrived = spread(stored[window], "tmpl", column)
        crossed = swapped(arrived, "trial", 0)
        kept_slab = jnp.where(held_trial == trial_index, arrived, crossed)
        slabs.append(kept_slab)
    live_mask, source, holder_slot, ranking = read_plan(partners, counts, per_device, width)
    slot_range = jnp.arange(per_device, dtype=jnp.int32)
    cap_range = jnp.arange(capacity, dtype=jnp.int32)
    outgoing = live_mask & (source == device)
    by_rank = outgoing[:, None, :] & (ranking[:, None, :] == cap_range[None, :, None])
    by_slot = holder_slot[:, :, None] == slot_range[None, None, :]
    selector = jnp.einsum("ecs,est->ect", by_rank.astype(jnp.float32), by_slot.astype(jnp.float32))
    selector = selector.reshape(width * capacity, per_device).astype(jnp.bfloat16)
    own_live = live_mask[device]
    incoming = source[device] * capacity + ranking[device]
    receiver = (
        incoming[:, None] == jnp.arange(width * capacity, dtype=jnp.int32)[None, :]
    ) & own_live[:, None]
    receiver = receiver.astype(jnp.bfloat16)
    split_at = bins_whole + tap_count
    own_planes = []
    for window in range(windows):
        halved = slabs[window][:, split_at:]
        own_planes.append(
            blocked_powers(weights, halved, tap_count, bins_half).astype(jnp.bfloat16)
        )
    outbound = jnp.dot(
        selector, jnp.concatenate(own_planes, axis=1), preferred_element_type=jnp.float32
    ).astype(jnp.bfloat16)
    inbound = lax.all_to_all(outbound, "tmpl", split_axis=0, concat_axis=0, tiled=True)
    borrowed = jnp.dot(receiver, inbound, preferred_element_type=jnp.float32).astype(jnp.bfloat16)
    partner_planes = [
        borrowed[:, window * bins_half : (window + 1) * bins_half] for window in range(windows)
    ]
    results = []
    for window in range(windows):
        direct = blocked_powers(weights, slabs[window][:, :split_at], tap_count, bins_whole)
        stretched = jnp.repeat(partner_planes[window], 2, axis=1).astype(jnp.float32)
        summed = jnp.where(own_live[:, None], direct + stretched, jnp.float32(0.0))
        results.append(summed.astype(jnp.bfloat16))
    return jnp.stack(results)[:, None]


def solution(mesh):
    return jax.shard_map(
        body,
        mesh=mesh,
        in_specs=(
            P(None, "trial", "tmpl", None, None),
            P(None, "trial", "tmpl", None, None),
            P("tmpl", None, None),
            P(),
            P(),
            P(),
        ),
        out_specs=P(None, "trial", "tmpl", None),
        check_vma=False,
    )
```

profile of v0, /device:TPU:0, one launch (start us, length us, event | category | flops | bytes accessed | tf_op | source)
XLA Modules:
  0.0 1202.3 jit_solution(11948855770315759957)
XLA Ops:
  19.5 104.2 %all-reduce.3.cloned.1.call-done = (bf16[2,25600]{1,0:T(2,128)(2,1)}, bf16[2,25600]{1,0:T(2,128)(2,1)}) async-done(((bf16[2,25600]{1,0:T(2,128)(2,1)}, bf16[2,25600]{1,0:T(2,128)(2,1)}), (bf16[2,25600]{1,0:T(2,128)(2,1)}, bf16[2,25600]{1,0:T(2,128)(2,1)})) %all-reduce.3.cloned.1.call-update) | async-done | bytes 204816 | tf_op jit(solution)/shard_map/psum | solution.py:9
  127.6 163.0 %while.54 = (s32[]{:T(128)}, bf16[16,8192]{1,0:T(8,128)(2,1)S(1)}, bf16[2,8704]{1,0:T(2,128)(2,1)S(1)}, bf16[32,1024]{1,0:T(8,128)(2,1)S(1)}, s32[]{:T(128)}, /*index=5*/s32[]{:T(128)}, s32[]{:T(128)}, s32[]{:T(128)}, s32[]{:T(128)}) while((s32[]{:T(128)}, bf16[16,8192]{1,0:T(8,128)(2,1)S(1)}, bf16[2,8704]{1,0:T(2,128)(2,1)S(1)}, ...), condition=%wide.region_8.9_spmd, body=%wide.region_7.8_spmd.sunk | while | flops 67158024 | bytes 37142724 | solution.py:49
  138.5 7.4 reshape.288
  179.3 7.4 reshape.288
  199.6 7.4 reshape.288
  220.0 7.4 reshape.288
  240.4 7.4 reshape.288
  260.8 7.4 reshape.288
  281.1 7.4 reshape.288
  291.3 168.0 %while.53 = (s32[]{:T(128)}, bf16[16,8192]{1,0:T(8,128)(2,1)}, bf16[2,8704]{1,0:T(2,128)(2,1)S(1)}, bf16[32,1024]{1,0:T(8,128)(2,1)S(1)}, s32[]{:T(128)}, /*index=5*/s32[]{:T(128)}, s32[]{:T(128)}, s32[]{:T(128)}, s32[]{:T(128)}) while((s32[]{:T(128)}, bf16[16,8192]{1,0:T(8,128)(2,1)}, bf16[2,8704]{1,0:T(2,128)(2,1)S(1)}, ...), condition=%wide.region_5.6_spmd, body=%wide.region_4.5_spmd.sunk | while | flops 67158024 | bytes 37142724 | solution.py:49
  323.6 7.4 reshape.286
  344.6 7.4 reshape.286
  365.5 7.4 reshape.286
  386.4 7.4 reshape.286
  428.3 7.4 reshape.286
  449.3 7.4 reshape.286
  470.2 335.3 %while.52 = (s32[]{:T(128)}, f32[16,16384]{1,0:T(8,128)}, bf16[2,16896]{1,0:T(2,128)(2,1)S(1)}, bf16[32,1024]{1,0:T(8,128)(2,1)S(1)}, s32[]{:T(128)}, /*index=5*/s32[]{:T(128)}, s32[]{:T(128)}, s32[]{:T(128)}, s32[]{:T(128)}) while((s32[]{:T(128)}, f32[16,16384]{1,0:T(8,128)}, bf16[2,16896]{1,0:T(2,128)(2,1)S(1)}, ...), condition=%wide.region_2.3_spmd, body=%wide.region_1.2_spmd.sunk | while | flops 67158024 | bytes 37142724 | solution.py:49
  481.1 7.4 reshape.284
  502.0 7.4 reshape.284
  543.9 7.4 reshape.284
  564.9 7.4 reshape.284
  806.5 335.4 %while.55 = (s32[]{:T(128)}, f32[16,16384]{1,0:T(8,128)}, bf16[2,16896]{1,0:T(2,128)(2,1)S(1)}, bf16[32,1024]{1,0:T(8,128)(2,1)S(1)}, s32[]{:T(128)}, /*index=5*/s32[]{:T(128)}, s32[]{:T(128)}, s32[]{:T(128)}, s32[]{:T(128)}) while((s32[]{:T(128)}, f32[16,16384]{1,0:T(8,128)}, bf16[2,16896]{1,0:T(2,128)(2,1)S(1)}, ...), condition=%wide.region_10.11_spmd, body=%wide.region_9.10_spmd.sunk | while | flops 67158024 | bytes 37142724 | solution.py:49
  1161.2 8.6 broadcast_in_dim.106
  1174.3 12.7 %fusion.9 = (bf16[1,16,16384]{1,2,0:T(8,128)(2,1)}, bf16[1,16,16384]{1,2,0:T(8,128)(2,1)}) fusion(f32[16,16384]{0,1:T(8,128)} %copy.47, f32[16,16384]{0,1:T(8,128)} %bitcast.147, pred[16]{0:T(512)(128)(4,1)S(1)} %copy-done.6, f32[16,16384]{0,1:T(8,128)S(1)} %bitcast.146, f32[16,16384]{0,1:T(8,128)} %bitcast.148), kind=kLoop, calls=%fused_computation.33 | loop fusion | flops 1572864 | bytes 5242896 | tf_op jit(solution)/shard_map/stack | solution.py:120
  (534 shorter events, 931.9 us)
Async XLA Ops:
  6.5 117.1 %all-reduce.3.cloned.1.call-start = ((), (), s32[]{:S(2)}) async-start(), calls=%async_computation.1 | async-start | bytes 409600 | tf_op jit(solution)/shard_map/psum | solution.py:9
  123.7 1.5 collective-permute-start.1
  124.2 1.7 collective-permute-start
  125.3 1.6 copy-start.2
  127.6 163.7 %slice-start.7 = ((bf16[2,25600]{1,0:T(2,128)(2,1)}), bf16[2,8704]{1,0:T(2,128)(2,1)S(1)}, s32[]{:S(2)}) async-start(bf16[2,25600]{1,0:T(2,128)(2,1)} %copy-done.3), calls=%async_computation.9 | async-start | bytes 69632 | tf_op jit(solution)/shard_map/slice | solution.py:102
  145.9 1.6 slice-start
  186.6 1.6 slice-start
  207.0 1.6 slice-start
  227.4 1.6 slice-start
  247.7 1.6 slice-start
  268.1 1.6 slice-start
  288.5 1.6 slice-start
  291.3 168.0 %copy-start.4 = (f32[16,1,16]{2,1,0:T(1,128)S(1)}, f32[16,1,16]{2,1,0:T(1,128)}, u32[]{:S(2)}) copy-start(f32[16,1,16]{2,1,0:T(1,128)} %fusion.16) | copy-start | bytes 3076
  351.9 1.6 slice-start.1
  372.9 1.6 slice-start.1
  459.3 10.8 slice-start.8
  463.3 689.3 %all-to-all-start = ((bf16[16,2,8192]{2,1,0:T(2,128)(2,1)}), bf16[16,2,8192]{2,1,0:T(2,128)(2,1)}, u32[]{:S(2)}, u32[]{:S(2)}) async-start(bf16[16,2,8192]{2,1,0:T(2,128)(2,1)} %reshape.273), calls=%async_computation | async-start | bytes 1048576 | tf_op jit(solution)/shard_map/all_to_all | solution.py:109
  470.2 336.4 %slice-start.6 = ((bf16[2,25600]{1,0:T(2,128)(2,1)}), bf16[2,16896]{1,0:T(2,128)(2,1)S(1)}, s32[]{:S(2)}) async-start(bf16[2,25600]{1,0:T(2,128)(2,1)} %copy-done.2), calls=%async_computation.8 | async-start | bytes 135168 | tf_op jit(solution)/shard_map/slice | solution.py:116
  1141.9 6.0 copy-start.1
  1147.9 7.2 copy-start.5
  1147.9 7.2 copy-start.6
  1161.2 8.6 copy-start
  1161.2 13.1 %slice-start.4 = ((s8[8388608]{0:T(1024)(128)(4,1)}), s8[4194304]{0:T(1024)(128)(4,1)S(1)}, s32[]{:S(2)}) async-start(s8[8388608]{0:T(1024)(128)(4,1)} %bitcast.145), calls=%async_computation.6 | async-start | bytes 8388608
  1169.8 4.5 slice-start.5
  (40 other events, 62.7 us)
Sparse Core Ops, SparseCore 0:
  14.6 109.0 all-reduce.2
where the time goes:
time: 1210 us; the launch traced here: 1200 us
  local copies, waits for them, and re-layouts  999 us (83%)
  waiting for transfers between devices  105 us (9%)
  other arithmetic  46.9 us (4%)
  matrix products  25.1 us (2%)
  between operations  17.9 us (1%)
    reshape x48, local copies, waits for them, and re-layouts, hankel_rows(): repeated[:, :tap_count * (length + 1)].reshape(2, tap_count, length + 1)  353 us
    while x144, local copies, waits for them, and re-layouts  313 us
    slice x48, local copies, waits for them, and re-layouts, hankel_rows(): repeated[:, :tap_count * (length + 1)].reshape(2, tap_count, length + 1)  209 us
    psum x1, waiting for transfers between devices, spread(): return lax.psum(block, axis)  104 us
    slice x96, local copies, waits for them, and re-layouts, hankel_rows(): return skewed[:, :, :columns].reshape(2 * tap_count, columns)  76.3 us
    dynamic_update_slice x48, other arithmetic, add_block(): return lax.dynamic_update_slice_in_dim(result, values, first_bin, 1)  25.8 us
  transfers between devices with their start and end apart: 4, of which 3 were waited for; matrix products, arithmetic and copies ran while one was open for 53% of the time, Pallas kernels for 0%

commit v1 on v0

v1 whole, which is shorter than its diff:
```python
import functools

import jax
import jax.numpy as jnp
from jax import lax
from jax.experimental import pallas as pl
from jax.experimental.pallas import tpu as pltpu
from jax.sharding import PartitionSpec as P

LANES = 128
TILE = 16
MESH = pl.DeviceIdType.MESH


def toeplitz_into(target, slot, chunk_rows, chunks, lower):
    for part in range(2):
        previous = jnp.zeros((LANES, LANES), jnp.float32)
        for number in range(chunks + 1):
            if number < chunks:
                row = part * chunks + number
                spread = jnp.broadcast_to(chunk_rows[row : row + 1], (LANES, LANES))
                current = pltpu.roll(spread, 0, 1, stride=1, stride_axis=0)
            else:
                current = jnp.zeros((LANES, LANES), jnp.float32)
            block = jnp.where(lower, current, previous)
            target[slot, pl.ds(number * LANES, LANES), pl.ds(part * LANES, LANES)] = block.astype(
                jnp.bfloat16
            )
            previous = current


def kernel(
    plan,
    owners_ref,
    counts_ref,
    partners_ref,
    stored_ref,
    taps_ref,
    out_ref,
    candidates,
    chosen,
    gathered,
    widened,
    send_taps,
    recv_taps,
    flipped,
    own_toeplitz,
    partner_toeplitz,
    whole_rows,
    half_rows,
    planes,
    totals,
    piece_send,
    piece_recv,
    chosen_send,
    chosen_recv,
    taps_send,
    taps_recv,
):
    width, trials, per, chunks, windows, whole_blocks, half_blocks, piece_rows, hubs = plan
    devices = width * trials
    trial = lax.axis_index("trial")
    column = lax.axis_index("tmpl")
    me = column * trials + trial
    channel_rows = whole_blocks + half_blocks + 2 * chunks
    window_rows = 2 * channel_rows

    def place(flat):
        return (lax.rem(flat, trials), flat // trials)

    def hub_device(hub):
        return hub * devices // hubs

    my_hub = (me * hubs + devices - 1) // devices
    is_hub = hub_device(my_hub) == me
    my_rows = pl.ds(pl.multiple_of(my_hub * piece_rows, TILE), piece_rows)

    barrier = pltpu.get_barrier_semaphore()

    @pl.loop(1, devices)
    def _(step):
        pl.semaphore_signal(
            barrier, inc=1, device_id=place(lax.rem(me + step, devices)), device_id_type=MESH
        )

    pl.semaphore_wait(barrier, devices - 1)

    def piece_copy(hub):
        return pltpu.make_async_remote_copy(
            src_ref=stored_ref.at[pl.ds(pl.multiple_of(hub * piece_rows, TILE), piece_rows)],
            dst_ref=candidates.at[me],
            send_sem=piece_send.at[hub],
            recv_sem=piece_recv.at[me],
            device_id=place(hub_device(hub)),
            device_id_type=MESH,
        )

    @pl.loop(0, hubs)
    def _(step):
        hub = lax.rem(my_hub + step, hubs)

        @pl.when(hub_device(hub) != me)
        def _():
            piece_copy(hub).start()

    @pl.when(is_hub)
    def _():
        candidates[me] = stored_ref[my_rows, :]

    row_number = lax.broadcasted_iota(jnp.int32, (LANES, LANES), 0)
    lane_number = lax.broadcasted_iota(jnp.int32, (LANES, LANES), 1)
    lower = row_number >= lane_number
    flip = ((row_number + lane_number) % LANES == 0).astype(jnp.bfloat16)
    flipped[...] = jnp.dot(taps_ref[...], flip, preferred_element_type=jnp.float32).reshape(
        per, 2 * chunks, LANES
    )

    first = column * per

    @pl.loop(0, width)
    def _(receiver):
        slot = jnp.int32(0)
        for position in range(per):
            named = partners_ref[receiver * per + position] - first
            slot = jnp.where((named >= 0) & (named < per), named, slot)
        rows = flipped[slot]
        send_taps[receiver] = jnp.concatenate([rows, rows], axis=0).astype(jnp.bfloat16)

    def taps_copy(receiver):
        return pltpu.make_async_remote_copy(
            src_ref=send_taps.at[receiver],
            dst_ref=recv_taps.at[column],
            send_sem=taps_send.at[receiver],
            recv_sem=taps_recv.at[column],
            device_id=(trial, receiver),
            device_id_type=MESH,
        )

    @pl.loop(1, width)
    def _(step):
        taps_copy(lax.rem(column + step, width)).start()

    recv_taps[column] = send_taps[column]

    @pl.loop(0, per)
    def _(slot):
        toeplitz_into(own_toeplitz, slot, flipped[slot], chunks, lower)

    def chosen_copy(target):
        return pltpu.make_async_remote_copy(
            src_ref=chosen.at[lax.rem(target, trials)],
            dst_ref=gathered.at[my_rows],
            send_sem=chosen_send.at[target],
            recv_sem=chosen_recv.at[my_hub],
            device_id=place(target),
            device_id_type=MESH,
        )

    @pl.when(is_hub)
    def _():
        @pl.loop(1, devices)
        def _(step):
            other = lax.rem(me + step, devices)
            pltpu.make_async_remote_copy(
                src_ref=candidates.at[other],
                dst_ref=candidates.at[other],
                send_sem=piece_send.at[0],
                recv_sem=piece_recv.at[other],
                device_id=place(other),
                device_id_type=MESH,
            ).wait_recv()

        for which in range(trials):
            for part in range(piece_rows // TILE):
                window = (my_hub * piece_rows + part * TILE) // window_rows
                owner = owners_ref[window, which]
                source = lax.rem(owner, width) * trials + owner // width
                piece = candidates[source]
                chosen[which, pl.ds(part * TILE, TILE), :] = piece[
                    part * TILE : (part + 1) * TILE
                ]

        @pl.loop(1, devices)
        def _(step):
            chosen_copy(lax.rem(me + step, devices)).start()

        gathered[my_rows, :] = chosen[trial]

    @pl.loop(1, width)
    def _(step):
        other = lax.rem(column + step, width)
        pltpu.make_async_remote_copy(
            src_ref=recv_taps.at[other],
            dst_ref=recv_taps.at[other],
            send_sem=taps_send.at[0],
            recv_sem=taps_recv.at[other],
            device_id=(trial, other),
            device_id_type=MESH,
        ).wait_recv()

    @pl.loop(0, per)
    def _(slot):
        source = jnp.maximum(partners_ref[first + slot], 0) // per
        rows = recv_taps[source].astype(jnp.float32)
        toeplitz_into(partner_toeplitz, slot, rows, chunks, lower)

    @pl.loop(0, hubs)
    def _(hub):
        @pl.when(hub_device(hub) != me)
        def _():
            piece = gathered.at[pl.ds(pl.multiple_of(hub * piece_rows, TILE), piece_rows)]
            pltpu.make_async_remote_copy(
                src_ref=piece,
                dst_ref=piece,
                send_sem=chosen_send.at[0],
                recv_sem=chosen_recv.at[hub],
                device_id=place(hub_device(hub)),
                device_id_type=MESH,
            ).wait_recv()

    widened[...] = gathered[...].astype(jnp.float32)
    for pair in range(2 * windows):
        for number in range(chunks + 1):
            lanes = pl.ds(number * LANES, LANES)
            begin = pair * channel_rows + number
            whole_rows[pl.ds(pair * whole_blocks, whole_blocks), lanes] = widened[
                pl.ds(begin, whole_blocks), :
            ].astype(jnp.bfloat16)
            begin += whole_blocks + chunks
            half_rows[pl.ds(pair * half_blocks, half_blocks), lanes] = widened[
                pl.ds(begin, half_blocks), :
            ].astype(jnp.bfloat16)

    def powers_of(rows_ref, matrix, blocks):
        product = jnp.dot(rows_ref[...], matrix, preferred_element_type=jnp.float32)
        result = []
        for window in range(windows):
            real = product[2 * window * blocks : (2 * window + 1) * blocks]
            imag = product[(2 * window + 1) * blocks : (2 * window + 2) * blocks]
            re = real[:, :LANES] - imag[:, LANES:]
            im = real[:, LANES:] + imag[:, :LANES]
            result.append(re * re + im * im)
        return result

    plane_rows = windows * half_blocks

    @pl.loop(0, per)
    def _(slot):
        values = powers_of(half_rows, partner_toeplitz[slot], half_blocks)
        planes[slot] = jnp.concatenate(values, axis=0).astype(jnp.bfloat16)

    doubling_row = lax.broadcasted_iota(jnp.int32, (LANES, 2 * LANES), 0)
    doubling_lane = lax.broadcasted_iota(jnp.int32, (LANES, 2 * LANES), 1)
    doubling = (doubling_row == doubling_lane // 2).astype(jnp.bfloat16)

    @pl.loop(0, per)
    def _(slot):
        doubled = jnp.dot(planes[slot], doubling, preferred_element_type=jnp.float32)
        for window in range(windows):
            base = (window * per + slot) * whole_blocks
            part = doubled[window * half_blocks : (window + 1) * half_blocks]
            for side in range(2):
                totals[pl.ds(base + side, half_blocks, stride=2), :] = part[
                    :, side * LANES : (side + 1) * LANES
                ]

    live = jnp.full((whole_blocks, LANES), counts_ref[column], jnp.int32)

    @pl.loop(0, per)
    def _(slot):
        values = powers_of(whole_rows, own_toeplitz[slot], whole_blocks)
        for window in range(windows):
            base = pl.multiple_of((window * per + slot) * whole_blocks, 8)
            rows = pl.ds(base, whole_blocks)
            totals[rows, :] = jnp.where(live > slot, values[window] + totals[rows, :], 0.0)

    for window in range(windows):
        for block in range(whole_blocks):
            rows = pl.ds(window * per * whole_blocks + block, per, stride=whole_blocks)
            out_ref[window, :, pl.ds(block * LANES, LANES)] = totals[rows, :].astype(jnp.bfloat16)

    @pl.loop(0, hubs)
    def _(hub):
        @pl.when(hub_device(hub) != me)
        def _():
            piece_copy(hub).wait_send()

    @pl.loop(1, width)
    def _(step):
        taps_copy(lax.rem(column + step, width)).wait_send()

    @pl.when(is_hub)
    def _():
        @pl.loop(1, devices)
        def _(step):
            chosen_copy(lax.rem(me + step, devices)).wait_send()


def body(spectra, half_spectra, kernels, owners, counts, partners):
    width = lax.axis_size("tmpl")
    trials = lax.axis_size("trial")
    devices = width * trials
    per, _, taps = kernels.shape
    windows = spectra.shape[0]
    chunks = taps // LANES
    whole_bins = spectra.shape[4] - taps
    whole_blocks = whole_bins // LANES
    half_blocks = (half_spectra.shape[4] - taps) // LANES
    stored = jnp.concatenate([spectra[:, 0, 0], half_spectra[:, 0, 0]], axis=2)
    stored = stored.reshape(-1, LANES)
    tap_rows = kernels.reshape(-1, LANES)
    rows = stored.shape[0]
    tiles = rows // TILE
    piece_tiles = -(-tiles // devices)
    hubs = tiles // piece_tiles
    piece_rows = piece_tiles * TILE
    plan = (width, trials, per, chunks, windows, whole_blocks, half_blocks, piece_rows, hubs)
    span = (chunks + 1) * LANES
    bf16, f32 = jnp.bfloat16, jnp.float32
    dma = pltpu.SemaphoreType.DMA
    smem = pl.BlockSpec(memory_space=pltpu.SMEM)
    vmem = pl.BlockSpec(memory_space=pltpu.VMEM)
    flops = 4 * per * 2 * span * windows * LANES * (whole_blocks + half_blocks)
    powers = pl.pallas_call(
        functools.partial(kernel, plan),
        out_shape=jax.ShapeDtypeStruct((windows, per, whole_bins), bf16),
        in_specs=[smem, smem, smem, vmem, vmem],
        out_specs=vmem,
        scratch_shapes=[
            pltpu.VMEM((devices, piece_rows, LANES), bf16),
            pltpu.VMEM((trials, piece_rows, LANES), bf16),
            pltpu.VMEM((rows, LANES), bf16),
            pltpu.VMEM((rows, LANES), f32),
            pltpu.VMEM((width, 2 * TILE if 2 * chunks > TILE else TILE, LANES), bf16),
            pltpu.VMEM((width, 2 * TILE if 2 * chunks > TILE else TILE, LANES), bf16),
            pltpu.VMEM((per, 2 * chunks, LANES), f32),
            pltpu.VMEM((per, span, 2 * LANES), bf16),
            pltpu.VMEM((per, span, 2 * LANES), bf16),
            pltpu.VMEM((2 * windows * whole_blocks, span), bf16),
            pltpu.VMEM((2 * windows * half_blocks, span), bf16),
            pltpu.VMEM((per, windows * half_blocks, LANES), bf16),
            pltpu.VMEM((windows * per * whole_blocks, LANES), f32),
            dma((hubs,)),
            dma((devices,)),
            dma((devices,)),
            dma((hubs,)),
            dma((width,)),
            dma((width,)),
        ],
        compiler_params=pltpu.CompilerParams(
            collective_id=0, has_side_effects=True, vmem_limit_bytes=48 * 1024 * 1024
        ),
        cost_estimate=pl.CostEstimate(flops=flops, bytes_accessed=2 * powers_size(windows, per, whole_bins), transcendentals=0),
    )(owners, counts, partners, stored, tap_rows)
    return powers[:, None]


def powers_size(windows, per, bins):
    return windows * per * bins


def solution(mesh):
    return jax.shard_map(
        body,
        mesh=mesh,
        in_specs=(
            P(None, "trial", "tmpl", None, None),
            P(None, "trial", "tmpl", None, None),
            P("tmpl", None, None),
            P(),
            P(),
            P(),
        ),
        out_specs=P(None, "trial", "tmpl", None),
        check_vma=False,
    )
```

time: 1210 us -> 41.3 us (0.03)
  local copies, waits for them, and re-layouts: 999 us -> 2.42 us
  waiting for transfers between devices: 105 us -> 0 us
  other arithmetic: 46.9 us -> 1.13 us
  Pallas kernels: 0 us -> 37.1 us
  matrix products: 25.1 us -> 0 us
  between operations: 17.9 us -> 0.05 us
    reshape x49 -> x2, local copies, waits for them, and re-layouts: 354 us -> 0.91 us  [the longest x1 0.78 us: body(): tap_rows = kernels.reshape(-1, LANES)]
    while x146 -> x0, local copies, waits for them, and re-layouts: 324 us -> none
    slice x153 -> x0, local copies, waits for them, and re-layouts: 287 us -> none  [the longest x48 209 us: hankel_rows(): repeated[:, :tap_count * (length + 1)].reshape(2, tap_count, length + 1)]
    psum x1 -> x0, waiting for transfers between devices: 104 us -> none  [spread(): return lax.psum(block, axis)]
    pallas_call x0 -> x1, Pallas kernels: none -> 37.1 us  [body(): pl.pallas_call(functools.partial(kernel, plan), out_shape=jax.ShapeDtypeS...]
    dynamic_update_slice x48 -> x0, other arithmetic: 25.8 us -> none  [add_block(): return lax.dynamic_update_slice_in_dim(result, values, first_bin, 1)]
    dot_general x51 -> x0, matrix products: 25.1 us -> none  [the longest x48 22.3 us: power_rows(): product = jnp.dot(weights, stacked, preferred_element_type=jnp.float32)]
    broadcast_in_dim x3 -> x0, local copies, waits for them, and re-layouts: 13.7 us -> none  [the longest x2 13.1 us: body(): jnp.repeat(partner_planes[window], 2, axis=1).astype(jnp.float32)]
  transfers between devices with their start and end apart: 4 -> 0, of which waited for: 3 -> 0; matrix products, arithmetic and copies ran while one was open for 53% -> 0% of each run, Pallas kernels for 0% -> 0%
where the time goes in v1:
time: 41.3 us; the launch traced here: 40.7 us
  Pallas kernels  37.1 us (90%)
  local copies, waits for them, and re-layouts  2.42 us (6%)
  other arithmetic  1.13 us (3%)
    pallas_call x1, Pallas kernels, body(): pl.pallas_call(functools.partial(kernel, plan), out_shape=jax.ShapeDtypeS...  37.1 us
    unnamed x7, local copies, waits for them, and re-layouts  1.51 us
    concatenate x1, other arithmetic, body(): stored = jnp.concatenate([spectra[:, 0, 0], half_spectra[:, 0, 0]], axis=2)  1.13 us

profile of v1, /device:TPU:0, one launch (start us, length us, event | category | flops | bytes accessed | tf_op | source)
XLA Modules:
  0.0 40.7 jit_solution(8259046417515332993)
XLA Ops:
  0.0 0.8 %reshape.7.taps_ref = bf16[128,128]{1,0:T(8,128)(2,1)S(1)} reshape(bf16[16,2,512]{2,1,0:T(2,128)(2,1)} %param.8) | data formatting | bytes 65536 | tf_op jit(solution)/shard_map/reshape | solution.py:311
  0.8 1.1 %pad_maximum_fusion = bf16[2,2,25600]{2,1,0:T(2,128)(2,1)S(1)} fusion(bf16[2,2,8704]{2,1,0:T(2,128)(2,1)} %bitcast.7, bf16[2,2,16896]{2,1,0:T(2,128)(2,1)} %bitcast.6), kind=kLoop, calls=%fused_computation | loop fusion | flops 409600 | bytes 409600 | tf_op jit(solution)/shard_map/concatenate | solution.py:309
  1.9 0.0 copy-start
  1.9 0.0 copy-start.1
  1.9 0.0 copy-start.2
  2.0 0.1 reshape.6.stored_ref
  2.1 0.5 %copy-done = s32[2,2]{1,0:T(2,128)S(1)} copy-done((s32[2,2]{1,0:T(2,128)S(1)}, s32[2,2]{1,0:T(2,128)}, u32[]{:S(2)}) %copy-start) | copy-done | bytes 40
  2.6 0.0 copy-done.1
  2.6 0.0 copy-done.2
  2.6 37.1 %shard_map.64 = bf16[2,16,16384]{2,1,0:T(8,128)(2,1)S(1)} custom-call(s32[2,2]{1,0:T(2,128)S(1)} %copy-done, s32[16]{0:T(128)S(1)} %copy-done.2, s32[256]{0:T(256)S(1)} %copy-done.1, bf16[800,128]{1,0:T(8,128)(2,1)S(1)} %reshape.6.stored_ref, bf16[128,128]{1,0:T(8,128)(2,1)S(1)} %reshape.7.taps_ref), custom_call_target="tpu_custom_call" | custom-call | flops 4026531840 | bytes 1048576 | tf_op jit(solution)/shard_map/pallas_call | solution.py:324
  39.7 1.0 %copy.9 = bf16[2,1,16,16384]{3,2,1,0:T(8,128)(2,1)} copy(bf16[2,1,16,16384]{3,2,1,0:T(8,128)(2,1)S(1)} %bitcast.5) | data formatting | bytes 2097152
Async XLA Ops:
  1.9 0.7 %copy-start = (s32[2,2]{1,0:T(2,128)S(1)}, s32[2,2]{1,0:T(2,128)}, u32[]{:S(2)}) copy-start(s32[2,2]{1,0:T(2,128)} %owners_ref.1) | copy-start | bytes 52
  1.9 0.7 %copy-start.1 = (s32[256]{0:T(256)S(1)}, s32[256]{0:T(256)}, u32[]{:S(2)}) copy-start(s32[256]{0:T(256)} %partners_ref.1) | copy-start | bytes 3076
  1.9 0.7 %copy-start.2 = (s32[16]{0:T(128)S(1)}, s32[16]{0:T(128)}, u32[]{:S(2)}) copy-start(s32[16]{0:T(128)} %counts_ref.1) | copy-start | bytes 196

commit v2 on v1

--- a/solution.py
+++ b/solution.py
@@ -17,7 +17,7 @@
         previous = jnp.zeros((LANES, LANES), jnp.float32)
         for number in range(chunks + 1):
             if number < chunks:
-                row = part * chunks + number
+                row = 2 * number + part
                 spread = jnp.broadcast_to(chunk_rows[row : row + 1], (LANES, LANES))
                 current = pltpu.roll(spread, 0, 1, stride=1, stride_axis=0)
             else:
@@ -34,9 +34,11 @@
     owners_ref,
     counts_ref,
     partners_ref,
-    stored_ref,
+    spectra_ref,
+    half_ref,
     taps_ref,
     out_ref,
+    stored_ref,
     candidates,
     chosen,
     gathered,
@@ -49,6 +51,7 @@
     whole_rows,
     half_rows,
     planes,
+    doubles,
     totals,
     piece_send,
     piece_recv,
@@ -83,6 +86,15 @@
             barrier, inc=1, device_id=place(lax.rem(me + step, devices)), device_id_type=MESH
         )
 
+    for window in range(windows):
+        for number in range(channel_rows):
+            held, lane = spectra_ref, number * LANES
+            if number >= whole_blocks + chunks:
+                held, lane = half_ref, (number - whole_blocks - chunks) * LANES
+            rows = pl.ds(window * window_rows + number, 2, stride=channel_rows)
+            widened[rows, :] = held[window, :, pl.ds(lane, LANES)].astype(jnp.float32)
+    stored_ref[...] = widened[...].astype(jnp.bfloat16)
+
     pl.semaphore_wait(barrier, devices - 1)
 
     def piece_copy(hub):
@@ -111,9 +123,11 @@
     lane_number = lax.broadcasted_iota(jnp.int32, (LANES, LANES), 1)
     lower = row_number >= lane_number
     flip = ((row_number + lane_number) % LANES == 0).astype(jnp.bfloat16)
-    flipped[...] = jnp.dot(taps_ref[...], flip, preferred_element_type=jnp.float32).reshape(
-        per, 2 * chunks, LANES
-    )
+    for number in range(chunks):
+        held = taps_ref[:, :, pl.ds(number * LANES, LANES)].astype(jnp.float32)
+        held = held.reshape(2 * per, LANES).astype(jnp.bfloat16)
+        turned = jnp.dot(held, flip, preferred_element_type=jnp.float32)
+        flipped[:, pl.ds(2 * number, 2), :] = turned.reshape(per, 2, LANES)
 
     first = column * per
 
@@ -142,7 +156,7 @@
 
     recv_taps[column] = send_taps[column]
 
-    @pl.loop(0, per)
+    @pl.loop(0, per, unroll=2)
     def _(slot):
         toeplitz_into(own_toeplitz, slot, flipped[slot], chunks, lower)
 
@@ -198,7 +212,7 @@
             device_id_type=MESH,
         ).wait_recv()
 
-    @pl.loop(0, per)
+    @pl.loop(0, per, unroll=2)
     def _(slot):
         source = jnp.maximum(partners_ref[first + slot], 0) // per
         rows = recv_taps[source].astype(jnp.float32)
@@ -244,7 +258,7 @@
 
     plane_rows = windows * half_blocks
 
-    @pl.loop(0, per)
+    @pl.loop(0, per, unroll=4)
     def _(slot):
         values = powers_of(half_rows, partner_toeplitz[slot], half_blocks)
         planes[slot] = jnp.concatenate(values, axis=0).astype(jnp.bfloat16)
@@ -253,30 +267,32 @@
     doubling_lane = lax.broadcasted_iota(jnp.int32, (LANES, 2 * LANES), 1)
     doubling = (doubling_row == doubling_lane // 2).astype(jnp.bfloat16)
 
-    @pl.loop(0, per)
+    @pl.loop(0, per, unroll=4)
     def _(slot):
         doubled = jnp.dot(planes[slot], doubling, preferred_element_type=jnp.float32)
         for window in range(windows):
             base = (window * per + slot) * whole_blocks
             part = doubled[window * half_blocks : (window + 1) * half_blocks]
             for side in range(2):
-                totals[pl.ds(base + side, half_blocks, stride=2), :] = part[
+                doubles[pl.ds(base + side, half_blocks, stride=2), :] = part[
                     :, side * LANES : (side + 1) * LANES
                 ]
 
+    pitch = per + 1
     live = jnp.full((whole_blocks, LANES), counts_ref[column], jnp.int32)
 
-    @pl.loop(0, per)
+    @pl.loop(0, per, unroll=2)
     def _(slot):
         values = powers_of(whole_rows, own_toeplitz[slot], whole_blocks)
         for window in range(windows):
             base = pl.multiple_of((window * per + slot) * whole_blocks, 8)
-            rows = pl.ds(base, whole_blocks)
-            totals[rows, :] = jnp.where(live > slot, values[window] + totals[rows, :], 0.0)
+            total = values[window] + doubles[pl.ds(base, whole_blocks), :]
+            rows = pl.ds(window * whole_blocks * pitch + slot, whole_blocks, stride=pitch)
+            totals[rows, :] = jnp.where(live > slot, total, 0.0)
 
     for window in range(windows):
         for block in range(whole_blocks):
-            rows = pl.ds(window * per * whole_blocks + block, per, stride=whole_blocks)
+            rows = pl.ds((window * whole_blocks + block) * pitch, per)
             out_ref[window, :, pl.ds(block * LANES, LANES)] = totals[rows, :].astype(jnp.bfloat16)
 
     @pl.loop(0, hubs)
@@ -306,10 +322,7 @@
     whole_bins = spectra.shape[4] - taps
     whole_blocks = whole_bins // LANES
     half_blocks = (half_spectra.shape[4] - taps) // LANES
-    stored = jnp.concatenate([spectra[:, 0, 0], half_spectra[:, 0, 0]], axis=2)
-    stored = stored.reshape(-1, LANES)
-    tap_rows = kernels.reshape(-1, LANES)
-    rows = stored.shape[0]
+    rows = windows * 2 * (whole_blocks + half_blocks + 2 * chunks)
     tiles = rows // TILE
     piece_tiles = -(-tiles // devices)
     hubs = tiles // piece_tiles
@@ -324,9 +337,10 @@
     powers = pl.pallas_call(
         functools.partial(kernel, plan),
         out_shape=jax.ShapeDtypeStruct((windows, per, whole_bins), bf16),
-        in_specs=[smem, smem, smem, vmem, vmem],
+        in_specs=[smem, smem, smem, vmem, vmem, vmem],
         out_specs=vmem,
         scratch_shapes=[
+            pltpu.VMEM((rows, LANES), bf16),
             pltpu.VMEM((devices, piece_rows, LANES), bf16),
             pltpu.VMEM((trials, piece_rows, LANES), bf16),
             pltpu.VMEM((rows, LANES), bf16),
@@ -340,6 +354,7 @@
             pltpu.VMEM((2 * windows * half_blocks, span), bf16),
             pltpu.VMEM((per, windows * half_blocks, LANES), bf16),
             pltpu.VMEM((windows * per * whole_blocks, LANES), f32),
+            pltpu.VMEM((windows * whole_blocks * (per + 1), LANES), f32),
             dma((hubs,)),
             dma((devices,)),
             dma((devices,)),
@@ -351,7 +366,7 @@
             collective_id=0, has_side_effects=True, vmem_limit_bytes=48 * 1024 * 1024
         ),
         cost_estimate=pl.CostEstimate(flops=flops, bytes_accessed=2 * powers_size(windows, per, whole_bins), transcendentals=0),
-    )(owners, counts, partners, stored, tap_rows)
+    )(owners, counts, partners, spectra[:, 0, 0], half_spectra[:, 0, 0], kernels)
     return powers[:, None]
 
 

time: 41.3 us -> 35.8 us (0.87)
  Pallas kernels: 37.1 us -> 30.9 us
  local copies, waits for them, and re-layouts: 2.42 us -> 4.21 us
  other arithmetic: 1.13 us -> 0 us
    pallas_call x1, Pallas kernels: 37.1 us -> 30.9 us  [body(): pl.pallas_call(functools.partial(kernel, plan), out_shape=jax.ShapeDtypeS...]
    unnamed x7 -> x13, local copies, waits for them, and re-layouts: 1.51 us -> 4.21 us
    concatenate x1 -> x0, other arithmetic: 1.13 us -> none  [body(): stored = jnp.concatenate([spectra[:, 0, 0], half_spectra[:, 0, 0]], axis=2)]
    reshape x2 -> x0, local copies, waits for them, and re-layouts: 0.91 us -> none  [the longest x1 0.78 us: body(): tap_rows = kernels.reshape(-1, LANES)]
where the time goes in v2:
time: 35.8 us; the launch traced here: 35.1 us
  Pallas kernels  30.9 us (86%)
  local copies, waits for them, and re-layouts  4.21 us (12%)
    pallas_call x1, Pallas kernels, body(): pl.pallas_call(functools.partial(kernel, plan), out_shape=jax.ShapeDtypeS...  30.9 us
    unnamed x13, local copies, waits for them, and re-layouts  4.21 us

profile of v2, /device:TPU:0, one launch (start us, length us, event | category | flops | bytes accessed | tf_op | source)
XLA Modules:
  0.0 35.1 jit_solution(14131186076211582822)
XLA Ops:
  0.0 0.0 copy-start.4
  0.0 0.0 copy-start.3
  0.0 0.0 copy-start.5
  0.0 0.7 %copy-done.4 = s32[256]{0:T(256)S(1)} copy-done((s32[256]{0:T(256)S(1)}, s32[256]{0:T(256)}, u32[]{:S(2)}) %copy-start.4) | copy-done | bytes 1048
  0.7 0.0 copy-done.3
  0.7 0.0 copy-done.5
  0.7 0.0 copy-start
  0.7 0.9 %copy-done = bf16[2,1,1,2,16896]{4,3,2,1,0:T(2,128)(2,1)S(1)} copy-done((bf16[2,1,1,2,16896]{4,3,2,1,0:T(2,128)(2,1)S(1)}, bf16[2,1,1,2,16896]{4,3,2,1,0:T(2,128)(2,1)}, u32[]{:S(2)}) %copy-start) | copy-done | bytes 135192
  1.6 0.0 copy-start.1
  1.6 0.9 %copy-done.1 = bf16[2,1,1,2,8704]{4,3,2,1,0:T(2,128)(2,1)S(1)} copy-done((bf16[2,1,1,2,8704]{4,3,2,1,0:T(2,128)(2,1)S(1)}, bf16[2,1,1,2,8704]{4,3,2,1,0:T(2,128)(2,1)}, u32[]{:S(2)}) %copy-start.1) | copy-done | bytes 69656
  2.5 0.0 copy-start.2
  2.5 0.8 %copy-done.2 = bf16[16,2,512]{2,1,0:T(2,128)(2,1)S(1)} copy-done((bf16[16,2,512]{2,1,0:T(2,128)(2,1)S(1)}, bf16[16,2,512]{2,1,0:T(2,128)(2,1)}, u32[]{:S(2)}) %copy-start.2) | copy-done | bytes 32792
  3.2 30.9 %shard_map.64 = bf16[2,16,16384]{2,1,0:T(8,128)(2,1)S(1)} custom-call(s32[2,2]{1,0:T(2,128)S(1)} %copy-done.3, s32[16]{0:T(128)S(1)} %copy-done.5, s32[256]{0:T(256)S(1)} %copy-done.4, bf16[2,2,16896]{2,1,0:T(2,128)(2,1)S(1)} %bitcast.6, bf16[2,2,8704]{2,1,0:T(2,128)(2,1)S(1)} %bitcast.7, bf16[16,2,512]{2,1,0:T(2,128)(2,1)S(1)} %copy-done.2), custom_call_target="tpu_custom_call" | custom-call | flops 4026531840 | bytes 1048576 | tf_op jit(solution)/shard_map/pallas_call | solution.py:337
  34.2 1.0 %copy.9 = bf16[2,1,16,16384]{3,2,1,0:T(8,128)(2,1)} copy(bf16[2,1,16,16384]{3,2,1,0:T(8,128)(2,1)S(1)} %bitcast.5) | data formatting | bytes 2097152
Async XLA Ops:
  0.0 0.7 %copy-start.4 = (s32[256]{0:T(256)S(1)}, s32[256]{0:T(256)}, u32[]{:S(2)}) copy-start(s32[256]{0:T(256)} %partners_ref.1) | copy-start | bytes 3076
  0.0 0.7 %copy-start.3 = (s32[2,2]{1,0:T(2,128)S(1)}, s32[2,2]{1,0:T(2,128)}, u32[]{:S(2)}) copy-start(s32[2,2]{1,0:T(2,128)} %owners_ref.1) | copy-start | bytes 52
  0.0 0.7 %copy-start.5 = (s32[16]{0:T(128)S(1)}, s32[16]{0:T(128)}, u32[]{:S(2)}) copy-start(s32[16]{0:T(128)} %counts_ref.1) | copy-start | bytes 196
  0.7 0.9 %copy-start = (bf16[2,1,1,2,16896]{4,3,2,1,0:T(2,128)(2,1)S(1)}, bf16[2,1,1,2,16896]{4,3,2,1,0:T(2,128)(2,1)}, u32[]{:S(2)}) copy-start(bf16[2,1,1,2,16896]{4,3,2,1,0:T(2,128)(2,1)} %param.6) | copy-start | bytes 405508
  1.6 0.9 %copy-start.1 = (bf16[2,1,1,2,8704]{4,3,2,1,0:T(2,128)(2,1)S(1)}, bf16[2,1,1,2,8704]{4,3,2,1,0:T(2,128)(2,1)}, u32[]{:S(2)}) copy-start(bf16[2,1,1,2,8704]{4,3,2,1,0:T(2,128)(2,1)} %param.7) | copy-start | bytes 208900
  2.5 0.8 %copy-start.2 = (bf16[16,2,512]{2,1,0:T(2,128)(2,1)S(1)}, bf16[16,2,512]{2,1,0:T(2,128)(2,1)}, u32[]{:S(2)}) copy-start(bf16[16,2,512]{2,1,0:T(2,128)(2,1)} %taps_ref.1) | copy-start | bytes 98308

commit v3 on v2

v3 whole, which is shorter than its diff:
```python
import functools

import jax
import jax.numpy as jnp
from jax import lax
from jax.experimental import pallas as pl
from jax.experimental.pallas import tpu as pltpu
from jax.sharding import PartitionSpec as P

LANES = 128
TILE = 16
MESH = pl.DeviceIdType.MESH


def toeplitz_into(target, slot, chunk_rows, chunks, lower):
    for part in range(2):
        previous = jnp.zeros((LANES, LANES), jnp.float32)
        for number in range(chunks + 1):
            if number < chunks:
                row = 2 * number + part
                spread = jnp.broadcast_to(chunk_rows[row : row + 1], (LANES, LANES))
                current = pltpu.roll(spread, 0, 1, stride=1, stride_axis=0)
            else:
                current = jnp.zeros((LANES, LANES), jnp.float32)
            block = jnp.where(lower, current, previous)
            target[slot, pl.ds(number * LANES, LANES), pl.ds(part * LANES, LANES)] = block.astype(
                jnp.bfloat16
            )
            previous = current


class Stream:
    def __init__(self, devices, windows, blocks, chunks, shift):
        self.devices, self.windows, self.blocks, self.shift = devices, windows, blocks, shift
        self.channel_rows = blocks + chunks
        self.window_rows = 2 * self.channel_rows
        self.rows = windows * self.window_rows
        tiles = -(-self.rows // TILE)
        piece_tiles = -(-tiles // devices)
        self.hubs = -(-tiles // piece_tiles)
        self.piece_rows = piece_tiles * TILE
        self.padded = self.hubs * self.piece_rows

    def scratch(self, trials, span):
        bf16, f32, dma = jnp.bfloat16, jnp.float32, pltpu.SemaphoreType.DMA
        return [
            pltpu.VMEM((self.padded, LANES), bf16),
            pltpu.VMEM((self.devices, self.piece_rows, LANES), bf16),
            pltpu.VMEM((trials, self.piece_rows, LANES), bf16),
            pltpu.VMEM((self.padded, LANES), bf16),
            pltpu.VMEM((self.padded, LANES), f32),
            pltpu.VMEM((2 * self.windows * self.blocks, span), bf16),
            dma((self.hubs,)),
            dma((self.devices,)),
            dma((self.devices,)),
            dma((self.hubs,)),
        ]

    def bind(self, refs, trials, width, trial, me):
        (
            self.stored,
            self.candidates,
            self.chosen,
            self.gathered,
            self.widened,
            self.blocked,
            self.piece_send,
            self.piece_recv,
            self.chosen_send,
            self.chosen_recv,
        ) = refs
        self.trials, self.width, self.trial, self.me = trials, width, trial, me
        turned = lax.rem(me + self.shift, self.devices)
        self.my_hub = (turned * self.hubs + self.devices - 1) // self.devices
        self.is_hub = self.hub_device(self.my_hub) == me
        self.my_rows = self.piece(self.my_hub)

    def hub_device(self, hub):
        place = hub * self.devices // self.hubs
        return lax.rem(place + self.devices - self.shift, self.devices)

    def piece(self, hub):
        return pl.ds(pl.multiple_of(hub * self.piece_rows, TILE), self.piece_rows)

    def place(self, flat):
        return (lax.rem(flat, self.trials), flat // self.trials)

    def lay_out(self, held):
        for window in range(self.windows):
            for number in range(self.channel_rows):
                rows = pl.ds(window * self.window_rows + number, 2, stride=self.channel_rows)
                lanes = pl.ds(number * LANES, LANES)
                self.widened[rows, :] = held[window, :, lanes].astype(jnp.float32)
        rest = self.padded - self.rows
        if rest:
            self.widened[pl.ds(self.rows, rest), :] = jnp.zeros((rest, LANES), jnp.float32)
        self.stored[...] = self.widened[...].astype(jnp.bfloat16)

    def piece_copy(self, hub):
        return pltpu.make_async_remote_copy(
            src_ref=self.stored.at[self.piece(hub)],
            dst_ref=self.candidates.at[self.me],
            send_sem=self.piece_send.at[hub],
            recv_sem=self.piece_recv.at[self.me],
            device_id=self.place(self.hub_device(hub)),
            device_id_type=MESH,
        )

    def each_other_hub(self, act):
        @pl.loop(0, self.hubs)
        def _(step):
            hub = lax.rem(self.my_hub + step, self.hubs)

            @pl.when(self.hub_device(hub) != self.me)
            def _():
                act(hub)

    def each_other_device(self, act):
        @pl.loop(1, self.devices)
        def _(step):
            act(lax.rem(self.me + step, self.devices))

    def scatter(self):
        self.each_other_hub(lambda hub: self.piece_copy(hub).start())

        @pl.when(self.is_hub)
        def _():
            self.candidates[self.me] = self.stored[self.my_rows, :]

    def chosen_copy(self, target):
        return pltpu.make_async_remote_copy(
            src_ref=self.chosen.at[lax.rem(target, self.trials)],
            dst_ref=self.gathered.at[self.my_rows],
            send_sem=self.chosen_send.at[target],
            recv_sem=self.chosen_recv.at[self.my_hub],
            device_id=self.place(target),
            device_id_type=MESH,
        )

    def arrival(self, ref, send_sem, recv_sem, device):
        return pltpu.make_async_remote_copy(
            src_ref=ref,
            dst_ref=ref,
            send_sem=send_sem,
            recv_sem=recv_sem,
            device_id=self.place(device),
            device_id_type=MESH,
        )

    def choose(self, owners_ref):
        @pl.when(self.is_hub)
        def _():
            self.each_other_device(
                lambda other: self.arrival(
                    self.candidates.at[other],
                    self.piece_send.at[0],
                    self.piece_recv.at[other],
                    other,
                ).wait_recv()
            )
            number = lax.broadcasted_iota(jnp.int32, (self.piece_rows, LANES), 0)
            number = number + self.my_hub * self.piece_rows
            for which in range(self.trials):
                kept = None
                for window in range(self.windows):
                    owner = owners_ref[window, which]
                    source = lax.rem(owner, self.width) * self.trials + owner // self.width
                    held = self.candidates[source].astype(jnp.float32)
                    if window:
                        held = jnp.where(number >= window * self.window_rows, held, kept)
                    kept = held
                self.chosen[which] = kept.astype(jnp.bfloat16)

            self.each_other_device(lambda target: self.chosen_copy(target).start())
            self.gathered[self.my_rows, :] = self.chosen[self.trial]

    def collect(self, chunks):
        self.each_other_hub(
            lambda hub: self.arrival(
                self.gathered.at[self.piece(hub)],
                self.chosen_send.at[0],
                self.chosen_recv.at[hub],
                self.hub_device(hub),
            ).wait_recv()
        )
        self.widened[...] = self.gathered[...].astype(jnp.float32)
        for pair in range(2 * self.windows):
            for number in range(chunks + 1):
                begin = pair * self.channel_rows + number
                rows = pl.ds(pair * self.blocks, self.blocks)
                self.blocked[rows, pl.ds(number * LANES, LANES)] = self.widened[
                    pl.ds(begin, self.blocks), :
                ].astype(jnp.bfloat16)

    def finish(self):
        self.each_other_hub(lambda hub: self.piece_copy(hub).wait_send())

        @pl.when(self.is_hub)
        def _():
            self.each_other_device(lambda target: self.chosen_copy(target).wait_send())


def kernel(plan, *refs):
    width, trials, per, chunks, half, whole = plan
    operands, out_ref, refs = refs[:6], refs[6], refs[7:]
    locals_, refs = refs[:6], refs[6:]
    half_refs, whole_refs, refs = refs[:10], refs[10:20], refs[20:]
    owners_ref, counts_ref, partners_ref, spectra_ref, halved_ref, taps_ref = locals_
    (
        send_taps,
        recv_taps,
        flipped,
        own_toeplitz,
        partner_toeplitz,
        planes,
        doubles,
        totals,
        taps_send,
        taps_recv,
        local_sem,
    ) = refs
    windows, whole_blocks, half_blocks = whole.windows, whole.blocks, half.blocks
    devices = width * trials
    trial = lax.axis_index("trial")
    column = lax.axis_index("tmpl")
    me = column * trials + trial
    half.bind(half_refs, trials, width, trial, me)
    whole.bind(whole_refs, trials, width, trial, me)

    local_copies = [
        pltpu.make_async_copy(operands[number], locals_[number], local_sem.at[number])
        for number in range(6)
    ]
    for copy in local_copies:
        copy.start()

    barrier = pltpu.get_barrier_semaphore()

    @pl.loop(1, devices)
    def _(step):
        other = lax.rem(me + step, devices)
        pl.semaphore_signal(barrier, inc=1, device_id=whole.place(other), device_id_type=MESH)

    for copy in local_copies:
        copy.wait()
    half.lay_out(halved_ref)
    whole.lay_out(spectra_ref)

    row_number = lax.broadcasted_iota(jnp.int32, (LANES, LANES), 0)
    lane_number = lax.broadcasted_iota(jnp.int32, (LANES, LANES), 1)
    lower = row_number >= lane_number
    flip = ((row_number + lane_number) % LANES == 0).astype(jnp.bfloat16)
    for number in range(chunks):
        held = taps_ref[:, :, pl.ds(number * LANES, LANES)].astype(jnp.float32)
        held = held.reshape(2 * per, LANES).astype(jnp.bfloat16)
        turned = jnp.dot(held, flip, preferred_element_type=jnp.float32)
        flipped[:, pl.ds(2 * number, 2), :] = turned.reshape(per, 2, LANES)

    first = column * per

    @pl.loop(0, width)
    def _(receiver):
        slot = jnp.int32(0)
        for position in range(per):
            named = partners_ref[receiver * per + position] - first
            slot = jnp.where((named >= 0) & (named < per), named, slot)
        rows = flipped[slot]
        send_taps[receiver] = jnp.concatenate([rows, rows], axis=0).astype(jnp.bfloat16)

    def taps_copy(receiver):
        return pltpu.make_async_remote_copy(
            src_ref=send_taps.at[receiver],
            dst_ref=recv_taps.at[column],
            send_sem=taps_send.at[receiver],
            recv_sem=taps_recv.at[column],
            device_id=(trial, receiver),
            device_id_type=MESH,
        )

    pl.semaphore_wait(barrier, devices - 1)
    half.scatter()
    whole.scatter()

    @pl.loop(1, width)
    def _(step):
        taps_copy(lax.rem(column + step, width)).start()

    recv_taps[column] = send_taps[column]

    def build_own(begin, end):
        @pl.loop(begin, end, unroll=2)
        def _(slot):
            toeplitz_into(own_toeplitz, slot, flipped[slot], chunks, lower)

    build_own(0, per // 2)
    half.choose(owners_ref)
    build_own(per // 2, per)
    whole.choose(owners_ref)

    @pl.loop(1, width)
    def _(step):
        other = lax.rem(column + step, width)
        pltpu.make_async_remote_copy(
            src_ref=recv_taps.at[other],
            dst_ref=recv_taps.at[other],
            send_sem=taps_send.at[0],
            recv_sem=taps_recv.at[other],
            device_id=(trial, other),
            device_id_type=MESH,
        ).wait_recv()

    @pl.loop(0, per, unroll=2)
    def _(slot):
        source = jnp.maximum(partners_ref[first + slot], 0) // per
        rows = recv_taps[source].astype(jnp.float32)
        toeplitz_into(partner_toeplitz, slot, rows, chunks, lower)

    def powers_of(rows_ref, matrix, blocks):
        product = jnp.dot(rows_ref[...], matrix, preferred_element_type=jnp.float32)
        result = []
        for window in range(windows):
            real = product[2 * window * blocks : (2 * window + 1) * blocks]
            imag = product[(2 * window + 1) * blocks : (2 * window + 2) * blocks]
            re = real[:, :LANES] - imag[:, LANES:]
            im = real[:, LANES:] + imag[:, :LANES]
            result.append(re * re + im * im)
        return result

    half.collect(chunks)

    @pl.loop(0, per, unroll=4)
    def _(slot):
        values = powers_of(half.blocked, partner_toeplitz[slot], half_blocks)
        planes[slot] = jnp.concatenate(values, axis=0).astype(jnp.bfloat16)

    doubling_row = lax.broadcasted_iota(jnp.int32, (LANES, 2 * LANES), 0)
    doubling_lane = lax.broadcasted_iota(jnp.int32, (LANES, 2 * LANES), 1)
    doubling = (doubling_row == doubling_lane // 2).astype(jnp.bfloat16)

    @pl.loop(0, per, unroll=4)
    def _(slot):
        doubled = jnp.dot(planes[slot], doubling, preferred_element_type=jnp.float32)
        for window in range(windows):
            base = (window * per + slot) * whole_blocks
            part = doubled[window * half_blocks : (window + 1) * half_blocks]
            for side in range(2):
                doubles[pl.ds(base + side, half_blocks, stride=2), :] = part[
                    :, side * LANES : (side + 1) * LANES
                ]

    whole.collect(chunks)
    pitch = per + 1
    live = jnp.full((whole_blocks, LANES), counts_ref[column], jnp.int32)

    @pl.loop(0, per, unroll=2)
    def _(slot):
        values = powers_of(whole.blocked, own_toeplitz[slot], whole_blocks)
        for window in range(windows):
            base = pl.multiple_of((window * per + slot) * whole_blocks, 8)
            total = values[window] + doubles[pl.ds(base, whole_blocks), :]
            rows = pl.ds(window * whole_blocks * pitch + slot, whole_blocks, stride=pitch)
            totals[rows, :] = jnp.where(live > slot, total, 0.0)

    for window in range(windows):
        for block in range(whole_blocks):
            rows = pl.ds((window * whole_blocks + block) * pitch, per)
            out_ref[window, :, pl.ds(block * LANES, LANES)] = totals[rows, :].astype(jnp.bfloat16)

    @pl.loop(1, width)
    def _(step):
        taps_copy(lax.rem(column + step, width)).wait_send()

    half.finish()
    whole.finish()


def body(spectra, half_spectra, kernels, owners, counts, partners):
    width = lax.axis_size("tmpl")
    trials = lax.axis_size("trial")
    devices = width * trials
    per, _, taps = kernels.shape
    windows = spectra.shape[0]
    chunks = taps // LANES
    whole_bins = spectra.shape[4] - taps
    whole_blocks = whole_bins // LANES
    half_blocks = (half_spectra.shape[4] - taps) // LANES
    half = Stream(devices, windows, half_blocks, chunks, 0)
    whole = Stream(devices, windows, whole_blocks, chunks, 1)
    plan = (width, trials, per, chunks, half, whole)
    span = (chunks + 1) * LANES
    bf16, f32 = jnp.bfloat16, jnp.float32
    dma = pltpu.SemaphoreType.DMA
    operands = (owners, counts, partners, spectra[:, 0, 0], half_spectra[:, 0, 0], kernels)
    near = (pltpu.SMEM, pltpu.SMEM, pltpu.SMEM, pltpu.VMEM, pltpu.VMEM, pltpu.VMEM)
    hbm = pl.BlockSpec(memory_space=pltpu.HBM)
    tap_rows = -(-2 * chunks // TILE) * TILE * (2 if 2 * chunks % TILE == 0 else 1)
    flops = 4 * per * 2 * span * windows * LANES * (whole_blocks + half_blocks)
    powers = pl.pallas_call(
        functools.partial(kernel, plan),
        out_shape=jax.ShapeDtypeStruct((windows, per, whole_bins), bf16),
        in_specs=[hbm] * 6,
        out_specs=pl.BlockSpec(memory_space=pltpu.VMEM),
        scratch_shapes=[
            *[space(held.shape, held.dtype) for space, held in zip(near, operands)],
            *half.scratch(trials, span),
            *whole.scratch(trials, span),
            pltpu.VMEM((width, tap_rows, LANES), bf16),
            pltpu.VMEM((width, tap_rows, LANES), bf16),
            pltpu.VMEM((per, 2 * chunks, LANES), f32),
            pltpu.VMEM((per, span, 2 * LANES), bf16),
            pltpu.VMEM((per, span, 2 * LANES), bf16),
            pltpu.VMEM((per, windows * half_blocks, LANES), bf16),
            pltpu.VMEM((windows * per * whole_blocks, LANES), f32),
            pltpu.VMEM((windows * whole_blocks * (per + 1), LANES), f32),
            dma((width,)),
            dma((width,)),
            dma((6,)),
        ],
        compiler_params=pltpu.CompilerParams(
            collective_id=0, has_side_effects=True, vmem_limit_bytes=48 * 1024 * 1024
        ),
        cost_estimate=pl.CostEstimate(flops=flops, bytes_accessed=2 * windows * per * whole_bins, transcendentals=0),
    )(*operands)
    return powers[:, None]


def solution(mesh):
    return jax.shard_map(
        body,
        mesh=mesh,
        in_specs=(
            P(None, "trial", "tmpl", None, None),
            P(None, "trial", "tmpl", None, None),
            P("tmpl", None, None),
            P(),
            P(),
            P(),
        ),
        out_specs=P(None, "trial", "tmpl", None),
        check_vma=False,
    )
```

time: 35.8 us -> 34.2 us (0.955); the launches traced: 35.1 us -> 33.9 us
  Pallas kernels: 30.9 us -> 29.7 us
    pallas_call x1, Pallas kernels: 30.9 us -> 29.7 us  [body(): pl.pallas_call(functools.partial(kernel, plan), out_shape=jax.ShapeDtypeS...]
where the time goes in v3:
time: 34.2 us; the launch traced here: 33.9 us
  Pallas kernels  29.7 us (87%)
  local copies, waits for them, and re-layouts  4.21 us (12%)
    pallas_call x1, Pallas kernels, body(): pl.pallas_call(functools.partial(kernel, plan), out_shape=jax.ShapeDtypeS...  29.7 us
    unnamed x13, local copies, waits for them, and re-layouts  4.21 us

profile of v3, /device:TPU:0, one launch (start us, length us, event | category | flops | bytes accessed | tf_op | source)
XLA Modules:
  0.0 33.9 jit_solution(10248396715298561086)
XLA Ops:
  0.0 0.0 copy-start.4
  0.0 0.0 copy-start.3
  0.0 0.0 copy-start.5
  0.0 0.7 %copy-done.4 = s32[256]{0:T(256)S(1)} copy-done((s32[256]{0:T(256)S(1)}, s32[256]{0:T(256)}, u32[]{:S(2)}) %copy-start.4) | copy-done | bytes 1048
  0.7 0.0 copy-done.3
  0.7 0.0 copy-done.5
  0.7 0.0 copy-start
  0.7 0.9 %copy-done = bf16[2,1,1,2,16896]{4,3,2,1,0:T(2,128)(2,1)S(1)} copy-done((bf16[2,1,1,2,16896]{4,3,2,1,0:T(2,128)(2,1)S(1)}, bf16[2,1,1,2,16896]{4,3,2,1,0:T(2,128)(2,1)}, u32[]{:S(2)}) %copy-start) | copy-done | bytes 135192
  1.6 0.0 copy-start.1
  1.6 0.9 %copy-done.1 = bf16[2,1,1,2,8704]{4,3,2,1,0:T(2,128)(2,1)S(1)} copy-done((bf16[2,1,1,2,8704]{4,3,2,1,0:T(2,128)(2,1)S(1)}, bf16[2,1,1,2,8704]{4,3,2,1,0:T(2,128)(2,1)}, u32[]{:S(2)}) %copy-start.1) | copy-done | bytes 69656
  2.5 0.0 copy-start.2
  2.5 0.8 %copy-done.2 = bf16[16,2,512]{2,1,0:T(2,128)(2,1)S(1)} copy-done((bf16[16,2,512]{2,1,0:T(2,128)(2,1)S(1)}, bf16[16,2,512]{2,1,0:T(2,128)(2,1)}, u32[]{:S(2)}) %copy-start.2) | copy-done | bytes 32792
  3.2 29.7 %shard_map.64 = bf16[2,16,16384]{2,1,0:T(8,128)(2,1)S(1)} custom-call(s32[2,2]{1,0:T(2,128)S(1)} %copy-done.3, s32[16]{0:T(128)S(1)} %copy-done.5, s32[256]{0:T(256)S(1)} %copy-done.4, bf16[2,2,16896]{2,1,0:T(2,128)(2,1)S(1)} %bitcast.6, bf16[2,2,8704]{2,1,0:T(2,128)(2,1)S(1)} %bitcast.7, bf16[16,2,512]{2,1,0:T(2,128)(2,1)S(1)} %copy-done.2), custom_call_target="tpu_custom_call" | custom-call | flops 4026531840 | bytes 1048576 | tf_op jit(solution)/shard_map/pallas_call | solution.py:398
  32.9 1.0 %copy.9 = bf16[2,1,16,16384]{3,2,1,0:T(8,128)(2,1)} copy(bf16[2,1,16,16384]{3,2,1,0:T(8,128)(2,1)S(1)} %bitcast.5) | data formatting | bytes 2097152
Async XLA Ops:
  0.0 0.7 %copy-start.4 = (s32[256]{0:T(256)S(1)}, s32[256]{0:T(256)}, u32[]{:S(2)}) copy-start(s32[256]{0:T(256)} %refs_2_.1) | copy-start | bytes 3076
  0.0 0.7 %copy-start.3 = (s32[2,2]{1,0:T(2,128)S(1)}, s32[2,2]{1,0:T(2,128)}, u32[]{:S(2)}) copy-start(s32[2,2]{1,0:T(2,128)} %refs_0_.1) | copy-start | bytes 52
  0.0 0.7 %copy-start.5 = (s32[16]{0:T(128)S(1)}, s32[16]{0:T(128)}, u32[]{:S(2)}) copy-start(s32[16]{0:T(128)} %refs_1_.1) | copy-start | bytes 196
  0.7 0.9 %copy-start = (bf16[2,1,1,2,16896]{4,3,2,1,0:T(2,128)(2,1)S(1)}, bf16[2,1,1,2,16896]{4,3,2,1,0:T(2,128)(2,1)}, u32[]{:S(2)}) copy-start(bf16[2,1,1,2,16896]{4,3,2,1,0:T(2,128)(2,1)} %param.6) | copy-start | bytes 405508
  1.6 0.9 %copy-start.1 = (bf16[2,1,1,2,8704]{4,3,2,1,0:T(2,128)(2,1)S(1)}, bf16[2,1,1,2,8704]{4,3,2,1,0:T(2,128)(2,1)}, u32[]{:S(2)}) copy-start(bf16[2,1,1,2,8704]{4,3,2,1,0:T(2,128)(2,1)} %param.7) | copy-start | bytes 208900
  2.5 0.8 %copy-start.2 = (bf16[16,2,512]{2,1,0:T(2,128)(2,1)S(1)}, bf16[16,2,512]{2,1,0:T(2,128)(2,1)}, u32[]{:S(2)}) copy-start(bf16[16,2,512]{2,1,0:T(2,128)(2,1)} %refs_5_.1) | copy-start | bytes 98308

commit v4 on v3

--- a/solution.py
+++ b/solution.py
@@ -29,14 +29,17 @@
             previous = current
 
 
+SPREAD = 5
+
+
 class Stream:
-    def __init__(self, devices, windows, blocks, chunks, shift):
-        self.devices, self.windows, self.blocks, self.shift = devices, windows, blocks, shift
+    def __init__(self, group, windows, blocks, chunks, first_hub, most_hubs):
+        self.group, self.windows, self.blocks, self.first_hub = group, windows, blocks, first_hub
         self.channel_rows = blocks + chunks
         self.window_rows = 2 * self.channel_rows
         self.rows = windows * self.window_rows
         tiles = -(-self.rows // TILE)
-        piece_tiles = -(-tiles // devices)
+        piece_tiles = -(-tiles // most_hubs)
         self.hubs = -(-tiles // piece_tiles)
         self.piece_rows = piece_tiles * TILE
         self.padded = self.hubs * self.piece_rows
@@ -45,14 +48,17 @@
         bf16, f32, dma = jnp.bfloat16, jnp.float32, pltpu.SemaphoreType.DMA
         return [
             pltpu.VMEM((self.padded, LANES), bf16),
-            pltpu.VMEM((self.devices, self.piece_rows, LANES), bf16),
+            pltpu.VMEM((self.group, self.piece_rows, LANES), bf16),
+            pltpu.VMEM((trials, self.piece_rows, LANES), bf16),
+            pltpu.VMEM((trials, self.piece_rows, LANES), bf16),
             pltpu.VMEM((trials, self.piece_rows, LANES), bf16),
             pltpu.VMEM((self.padded, LANES), bf16),
             pltpu.VMEM((self.padded, LANES), f32),
             pltpu.VMEM((2 * self.windows * self.blocks, span), bf16),
             dma((self.hubs,)),
-            dma((self.devices,)),
-            dma((self.devices,)),
+            dma((self.group,)),
+            dma((2,)),
+            dma((self.group,)),
             dma((self.hubs,)),
         ]
 
@@ -61,29 +67,37 @@
             self.stored,
             self.candidates,
             self.chosen,
+            self.across,
+            self.settled,
             self.gathered,
             self.widened,
             self.blocked,
             self.piece_send,
             self.piece_recv,
+            self.swap_sem,
             self.chosen_send,
             self.chosen_recv,
         ) = refs
         self.trials, self.width, self.trial, self.me = trials, width, trial, me
-        turned = lax.rem(me + self.shift, self.devices)
-        self.my_hub = (turned * self.hubs + self.devices - 1) // self.devices
-        self.is_hub = self.hub_device(self.my_hub) == me
+        self.my_group = me // self.group
+        self.local = lax.rem(me, self.group)
+        back = pow(SPREAD, -1, self.group)
+        turn = lax.rem(self.local * back + self.group - self.first_hub, self.group)
+        self.is_hub = turn < self.hubs
+        self.my_hub = jnp.minimum(turn, self.hubs - 1)
         self.my_rows = self.piece(self.my_hub)
 
-    def hub_device(self, hub):
-        place = hub * self.devices // self.hubs
-        return lax.rem(place + self.devices - self.shift, self.devices)
+    def hub_local(self, hub):
+        return lax.rem((hub + self.first_hub) * SPREAD, self.group)
 
     def piece(self, hub):
         return pl.ds(pl.multiple_of(hub * self.piece_rows, TILE), self.piece_rows)
 
     def place(self, flat):
         return (lax.rem(flat, self.trials), flat // self.trials)
+
+    def near(self, local):
+        return self.place(self.my_group * self.group + local)
 
     def lay_out(self, held):
         for window in range(self.windows):
@@ -99,41 +113,41 @@
     def piece_copy(self, hub):
         return pltpu.make_async_remote_copy(
             src_ref=self.stored.at[self.piece(hub)],
-            dst_ref=self.candidates.at[self.me],
+            dst_ref=self.candidates.at[self.local],
             send_sem=self.piece_send.at[hub],
-            recv_sem=self.piece_recv.at[self.me],
-            device_id=self.place(self.hub_device(hub)),
+            recv_sem=self.piece_recv.at[self.local],
+            device_id=self.near(self.hub_local(hub)),
             device_id_type=MESH,
         )
 
     def each_other_hub(self, act):
         @pl.loop(0, self.hubs)
         def _(step):
-            hub = lax.rem(self.my_hub + step, self.hubs)
-
-            @pl.when(self.hub_device(hub) != self.me)
+            hub = lax.rem(self.local + step, self.hubs)
+
+            @pl.when(self.hub_local(hub) != self.local)
             def _():
                 act(hub)
 
     def each_other_device(self, act):
-        @pl.loop(1, self.devices)
+        @pl.loop(1, self.group)
         def _(step):
-            act(lax.rem(self.me + step, self.devices))
+            act(lax.rem(self.local + step, self.group))
 
     def scatter(self):
         self.each_other_hub(lambda hub: self.piece_copy(hub).start())
 
         @pl.when(self.is_hub)
         def _():
-            self.candidates[self.me] = self.stored[self.my_rows, :]
+            self.candidates[self.local] = self.stored[self.my_rows, :]
 
     def chosen_copy(self, target):
         return pltpu.make_async_remote_copy(
-            src_ref=self.chosen.at[lax.rem(target, self.trials)],
+            src_ref=self.settled.at[lax.rem(target, self.trials)],
             dst_ref=self.gathered.at[self.my_rows],
             send_sem=self.chosen_send.at[target],
             recv_sem=self.chosen_recv.at[self.my_hub],
-            device_id=self.place(target),
+            device_id=self.near(target),
             device_id_type=MESH,
         )
 
@@ -143,7 +157,29 @@
             dst_ref=ref,
             send_sem=send_sem,
             recv_sem=recv_sem,
-            device_id=self.place(device),
+            device_id=self.near(device),
+            device_id_type=MESH,
+        )
+
+    def by_window(self, take):
+        number = lax.broadcasted_iota(jnp.int32, (self.piece_rows, LANES), 0)
+        number = number + self.my_hub * self.piece_rows
+        kept = take(0)
+        for window in range(1, self.windows):
+            kept = jnp.where(number >= window * self.window_rows, take(window), kept)
+        return kept.astype(jnp.bfloat16)
+
+    def flat_owner(self, owners_ref, window, which):
+        owner = owners_ref[window, which]
+        return lax.rem(owner, self.width) * self.trials + owner // self.width
+
+    def swap_copy(self):
+        return pltpu.make_async_remote_copy(
+            src_ref=self.chosen,
+            dst_ref=self.across,
+            send_sem=self.swap_sem.at[0],
+            recv_sem=self.swap_sem.at[1],
+            device_id=self.place(lax.rem(self.me + self.group, 2 * self.group)),
             device_id_type=MESH,
         )
 
@@ -158,21 +194,31 @@
                     other,
                 ).wait_recv()
             )
-            number = lax.broadcasted_iota(jnp.int32, (self.piece_rows, LANES), 0)
-            number = number + self.my_hub * self.piece_rows
             for which in range(self.trials):
-                kept = None
-                for window in range(self.windows):
-                    owner = owners_ref[window, which]
-                    source = lax.rem(owner, self.width) * self.trials + owner // self.width
-                    held = self.candidates[source].astype(jnp.float32)
-                    if window:
-                        held = jnp.where(number >= window * self.window_rows, held, kept)
-                    kept = held
-                self.chosen[which] = kept.astype(jnp.bfloat16)
-
+
+                def take(window):
+                    source = lax.rem(self.flat_owner(owners_ref, window, which), self.group)
+                    return self.candidates[source].astype(jnp.float32)
+
+                self.chosen[which] = self.by_window(take)
+            self.swap_copy().start()
+
+    def settle(self, owners_ref):
+        @pl.when(self.is_hub)
+        def _():
+            self.swap_copy().wait()
+            shape = (self.piece_rows, LANES)
+            for which in range(self.trials):
+                mine = self.chosen[which].astype(jnp.float32)
+                theirs = self.across[which].astype(jnp.float32)
+
+                def take(window):
+                    holder = self.flat_owner(owners_ref, window, which) // self.group
+                    return jnp.where(jnp.full(shape, holder) == self.my_group, mine, theirs)
+
+                self.settled[which] = self.by_window(take)
             self.each_other_device(lambda target: self.chosen_copy(target).start())
-            self.gathered[self.my_rows, :] = self.chosen[self.trial]
+            self.gathered[self.my_rows, :] = self.settled[self.trial]
 
     def collect(self, chunks):
         self.each_other_hub(
@@ -180,7 +226,7 @@
                 self.gathered.at[self.piece(hub)],
                 self.chosen_send.at[0],
                 self.chosen_recv.at[hub],
-                self.hub_device(hub),
+                self.hub_local(hub),
             ).wait_recv()
         )
         self.widened[...] = self.gathered[...].astype(jnp.float32)
@@ -204,7 +250,7 @@
     width, trials, per, chunks, half, whole = plan
     operands, out_ref, refs = refs[:6], refs[6], refs[7:]
     locals_, refs = refs[:6], refs[6:]
-    half_refs, whole_refs, refs = refs[:10], refs[10:20], refs[20:]
+    half_refs, whole_refs, refs = refs[:13], refs[13:26], refs[26:]
     owners_ref, counts_ref, partners_ref, spectra_ref, halved_ref, taps_ref = locals_
     (
         send_taps,
@@ -220,7 +266,6 @@
         local_sem,
     ) = refs
     windows, whole_blocks, half_blocks = whole.windows, whole.blocks, half.blocks
-    devices = width * trials
     trial = lax.axis_index("trial")
     column = lax.axis_index("tmpl")
     me = column * trials + trial
@@ -236,10 +281,15 @@
 
     barrier = pltpu.get_barrier_semaphore()
 
-    @pl.loop(1, devices)
+    def greet(place):
+        pl.semaphore_signal(barrier, inc=1, device_id=place, device_id_type=MESH)
+
+    far_column = (1 - me // whole.group) * (width // 2)
+    whole.each_other_device(lambda other: greet(whole.near(other)))
+
+    @pl.loop(0, width // 2)
     def _(step):
-        other = lax.rem(me + step, devices)
-        pl.semaphore_signal(barrier, inc=1, device_id=whole.place(other), device_id_type=MESH)
+        greet((trial, far_column + step))
 
     for copy in local_copies:
         copy.wait()
@@ -277,7 +327,7 @@
             device_id_type=MESH,
         )
 
-    pl.semaphore_wait(barrier, devices - 1)
+    pl.semaphore_wait(barrier, whole.group - 1 + width // 2)
     half.scatter()
     whole.scatter()
 
@@ -294,8 +344,11 @@
 
     build_own(0, per // 2)
     half.choose(owners_ref)
-    build_own(per // 2, per)
+    build_own(per // 2, 3 * per // 4)
+    half.settle(owners_ref)
     whole.choose(owners_ref)
+    build_own(3 * per // 4, per)
+    whole.settle(owners_ref)
 
     @pl.loop(1, width)
     def _(step):
@@ -377,15 +430,16 @@
 def body(spectra, half_spectra, kernels, owners, counts, partners):
     width = lax.axis_size("tmpl")
     trials = lax.axis_size("trial")
-    devices = width * trials
+    group = width * trials // 2
     per, _, taps = kernels.shape
     windows = spectra.shape[0]
     chunks = taps // LANES
     whole_bins = spectra.shape[4] - taps
     whole_blocks = whole_bins // LANES
     half_blocks = (half_spectra.shape[4] - taps) // LANES
-    half = Stream(devices, windows, half_blocks, chunks, 0)
-    whole = Stream(devices, windows, whole_blocks, chunks, 1)
+    half_hubs = max(1, group * (half_blocks + chunks) // (whole_blocks + half_blocks + 2 * chunks))
+    half = Stream(group, windows, half_blocks, chunks, 0, half_hubs)
+    whole = Stream(group, windows, whole_blocks, chunks, half.hubs, group - half.hubs)
     plan = (width, trials, per, chunks, half, whole)
     span = (chunks + 1) * LANES
     bf16, f32 = jnp.bfloat16, jnp.float32
@@ -417,7 +471,7 @@
             dma((6,)),
         ],
         compiler_params=pltpu.CompilerParams(
-            collective_id=0, has_side_effects=True, vmem_limit_bytes=48 * 1024 * 1024
+            collective_id=0, has_side_effects=True, vmem_limit_bytes=56 * 1024 * 1024
         ),
         cost_estimate=pl.CostEstimate(flops=flops, bytes_accessed=2 * windows * per * whole_bins, transcendentals=0),
     )(*operands)

time: 34.2 us -> 32 us (0.936)
  local copies, waits for them, and re-layouts: 4.21 us -> 2.26 us
    unnamed x13 -> x1, local copies, waits for them, and re-layouts: 4.21 us -> 2.26 us
where the time goes in v4:
time: 32 us; the launch traced here: 31.8 us
  Pallas kernels  29.6 us (92%)
  local copies, waits for them, and re-layouts  2.26 us (7%)
    pallas_call x1, Pallas kernels, body(): pl.pallas_call(functools.partial(kernel, plan), out_shape=jax.ShapeDtypeS...  29.6 us
    unnamed x1, local copies, waits for them, and re-layouts  2.26 us

profile of v4, /device:TPU:0, one launch (start us, length us, event | category | flops | bytes accessed | tf_op | source)
XLA Modules:
  0.0 31.8 jit_solution(7579610664027731869)
XLA Ops:
  0.0 29.6 %shard_map.64 = bf16[2,16,16384]{2,1,0:T(8,128)(2,1)} custom-call(s32[2,2]{1,0:T(2,128)} %refs_0_.1, s32[16]{0:T(128)} %refs_1_.1, s32[256]{0:T(256)} %refs_2_.1, bf16[2,2,16896]{2,1,0:T(2,128)(2,1)} %bitcast.6, bf16[2,2,8704]{2,1,0:T(2,128)(2,1)} %bitcast.7, bf16[16,2,512]{2,1,0:T(2,128)(2,1)} %refs_5_.1), custom_call_target="tpu_custom_call" | custom-call | flops 4026531840 | bytes 1048576 | tf_op jit(solution)/shard_map/pallas_call | solution.py:452
  29.6 2.3 %copy.9 = bf16[2,1,16,16384]{3,2,1,0:T(8,128)(2,1)} copy(bf16[2,1,16,16384]{3,2,1,0:T(8,128)(2,1)} %bitcast.5) | data formatting | bytes 2097152

commit v5 on v4

--- a/solution.py
+++ b/solution.py
@@ -12,20 +12,24 @@
 MESH = pl.DeviceIdType.MESH
 
 
-def toeplitz_into(target, slot, chunk_rows, chunks, lower):
+def toeplitz_into(target, slot, chunk_rows, chunks, masks):
+    zero = jnp.zeros((TILE, LANES), jnp.bfloat16)
+    steps = LANES // TILE
     for part in range(2):
-        previous = jnp.zeros((LANES, LANES), jnp.float32)
+        previous = [zero] * steps
         for number in range(chunks + 1):
+            current = [zero] * steps
             if number < chunks:
                 row = 2 * number + part
-                spread = jnp.broadcast_to(chunk_rows[row : row + 1], (LANES, LANES))
-                current = pltpu.roll(spread, 0, 1, stride=1, stride_axis=0)
-            else:
-                current = jnp.zeros((LANES, LANES), jnp.float32)
-            block = jnp.where(lower, current, previous)
-            target[slot, pl.ds(number * LANES, LANES), pl.ds(part * LANES, LANES)] = block.astype(
-                jnp.bfloat16
-            )
+                spread = jnp.broadcast_to(chunk_rows[row : row + 1], (TILE, LANES))
+                turned = pltpu.roll(spread, 0, 1, stride=1, stride_axis=0).astype(jnp.bfloat16)
+                current = [turned] + [
+                    pltpu.roll(turned, step * TILE, 1) for step in range(1, steps)
+                ]
+            for step in range(steps):
+                block = jnp.where(masks[step], current[step], previous[step])
+                rows = pl.ds(number * LANES + step * TILE, TILE)
+                target[slot, rows, pl.ds(part * LANES, LANES)] = block
             previous = current
 
 
@@ -298,7 +302,10 @@
 
     row_number = lax.broadcasted_iota(jnp.int32, (LANES, LANES), 0)
     lane_number = lax.broadcasted_iota(jnp.int32, (LANES, LANES), 1)
-    lower = row_number >= lane_number
+    masks = [
+        row_number[step * TILE : (step + 1) * TILE] >= lane_number[:TILE]
+        for step in range(LANES // TILE)
+    ]
     flip = ((row_number + lane_number) % LANES == 0).astype(jnp.bfloat16)
     for number in range(chunks):
         held = taps_ref[:, :, pl.ds(number * LANES, LANES)].astype(jnp.float32)
@@ -340,7 +347,7 @@
     def build_own(begin, end):
         @pl.loop(begin, end, unroll=2)
         def _(slot):
-            toeplitz_into(own_toeplitz, slot, flipped[slot], chunks, lower)
+            toeplitz_into(own_toeplitz, slot, flipped[slot], chunks, masks)
 
     build_own(0, per // 2)
     half.choose(owners_ref)
@@ -366,7 +373,7 @@
     def _(slot):
         source = jnp.maximum(partners_ref[first + slot], 0) // per
         rows = recv_taps[source].astype(jnp.float32)
-        toeplitz_into(partner_toeplitz, slot, rows, chunks, lower)
+        toeplitz_into(partner_toeplitz, slot, rows, chunks, masks)
 
     def powers_of(rows_ref, matrix, blocks):
         product = jnp.dot(rows_ref[...], matrix, preferred_element_type=jnp.float32)

time: 32 us -> 32 us (level)
  no operation moved by 1% of the time
where the time goes in v5:
time: 32 us; the launch traced here: 31.8 us
  Pallas kernels  29.6 us (92%)
  local copies, waits for them, and re-layouts  2.26 us (7%)
    pallas_call x1, Pallas kernels, body(): pl.pallas_call(functools.partial(kernel, plan), out_shape=jax.ShapeDtypeS...  29.6 us
    unnamed x1, local copies, waits for them, and re-layouts  2.26 us

profile of v5, /device:TPU:0, one launch (start us, length us, event | category | flops | bytes accessed | tf_op | source)
XLA Modules:
  0.0 31.8 jit_solution(8196450628140757665)
XLA Ops:
  0.0 29.6 %shard_map.64 = bf16[2,16,16384]{2,1,0:T(8,128)(2,1)} custom-call(s32[2,2]{1,0:T(2,128)} %refs_0_.1, s32[16]{0:T(128)} %refs_1_.1, s32[256]{0:T(256)} %refs_2_.1, bf16[2,2,16896]{2,1,0:T(2,128)(2,1)} %bitcast.6, bf16[2,2,8704]{2,1,0:T(2,128)(2,1)} %bitcast.7, bf16[16,2,512]{2,1,0:T(2,128)(2,1)} %refs_5_.1), custom_call_target="tpu_custom_call" | custom-call | flops 4026531840 | bytes 1048576 | tf_op jit(solution)/shard_map/pallas_call | solution.py:459
  29.6 2.3 %copy.9 = bf16[2,1,16,16384]{3,2,1,0:T(8,128)(2,1)} copy(bf16[2,1,16,16384]{3,2,1,0:T(8,128)(2,1)} %bitcast.5) | data formatting | bytes 2097152

commit v6 on v5

--- a/solution.py
+++ b/solution.py
@@ -255,7 +255,7 @@
     operands, out_ref, refs = refs[:6], refs[6], refs[7:]
     locals_, refs = refs[:6], refs[6:]
     half_refs, whole_refs, refs = refs[:13], refs[13:26], refs[26:]
-    owners_ref, counts_ref, partners_ref, spectra_ref, halved_ref, taps_ref = locals_
+    owners_ref, counts_ref, partners_ref, taps_ref, spectra_ref, halved_ref = locals_
     (
         send_taps,
         recv_taps,
@@ -280,7 +280,7 @@
         pltpu.make_async_copy(operands[number], locals_[number], local_sem.at[number])
         for number in range(6)
     ]
-    for copy in local_copies:
+    for copy in reversed(local_copies):
         copy.start()
 
     barrier = pltpu.get_barrier_semaphore()
@@ -295,10 +295,15 @@
     def _(step):
         greet((trial, far_column + step))
 
-    for copy in local_copies:
+    local_copies[5].wait()
+    half.lay_out(halved_ref)
+    pl.semaphore_wait(barrier, whole.group - 1 + width // 2)
+    half.scatter()
+    local_copies[4].wait()
+    whole.lay_out(spectra_ref)
+    whole.scatter()
+    for copy in local_copies[:4]:
         copy.wait()
-    half.lay_out(halved_ref)
-    whole.lay_out(spectra_ref)
 
     row_number = lax.broadcasted_iota(jnp.int32, (LANES, LANES), 0)
     lane_number = lax.broadcasted_iota(jnp.int32, (LANES, LANES), 1)
@@ -333,10 +338,6 @@
             device_id=(trial, receiver),
             device_id_type=MESH,
         )
-
-    pl.semaphore_wait(barrier, whole.group - 1 + width // 2)
-    half.scatter()
-    whole.scatter()
 
     @pl.loop(1, width)
     def _(step):
@@ -451,7 +452,8 @@
     span = (chunks + 1) * LANES
     bf16, f32 = jnp.bfloat16, jnp.float32
     dma = pltpu.SemaphoreType.DMA
-    operands = (owners, counts, partners, spectra[:, 0, 0], half_spectra[:, 0, 0], kernels)
+    operands = (owners, counts, partners, kernels, spectra[:, 0, 0], half_spectra[:, 0, 0])
+    operands = tuple(pltpu.with_memory_space_constraint(held, pltpu.HBM) for held in operands)
     near = (pltpu.SMEM, pltpu.SMEM, pltpu.SMEM, pltpu.VMEM, pltpu.VMEM, pltpu.VMEM)
     hbm = pl.BlockSpec(memory_space=pltpu.HBM)
     tap_rows = -(-2 * chunks // TILE) * TILE * (2 if 2 * chunks % TILE == 0 else 1)
@@ -478,7 +480,7 @@
             dma((6,)),
         ],
         compiler_params=pltpu.CompilerParams(
-            collective_id=0, has_side_effects=True, vmem_limit_bytes=56 * 1024 * 1024
+            collective_id=0, has_side_effects=True, vmem_limit_bytes=48 * 1024 * 1024
         ),
         cost_estimate=pl.CostEstimate(flops=flops, bytes_accessed=2 * windows * per * whole_bins, transcendentals=0),
     )(*operands)

time: 32 us -> 29.1 us (0.909)
  Pallas kernels: 29.6 us -> 27.7 us
  local copies, waits for them, and re-layouts: 2.26 us -> 0.97 us
    pallas_call x1, Pallas kernels: 29.6 us -> 27.7 us  [body(): pl.pallas_call(functools.partial(kernel, plan), out_shape=jax.ShapeDtypeS...]
    unnamed x1, local copies, waits for them, and re-layouts: 2.26 us -> 0.97 us
where the time goes in v6:
time: 29.1 us; the launch traced here: 28.7 us
  Pallas kernels  27.7 us (95%)
  local copies, waits for them, and re-layouts  0.97 us (3%)
    pallas_call x1, Pallas kernels, body(): pl.pallas_call(functools.partial(kernel, plan), out_shape=jax.ShapeDtypeS...  27.7 us
    unnamed x1, local copies, waits for them, and re-layouts  0.97 us

profile of v6, /device:TPU:0, one launch (start us, length us, event | category | flops | bytes accessed | tf_op | source)
XLA Modules:
  0.0 28.7 jit_solution(6677595011912408781)
XLA Ops:
  0.0 27.7 %shard_map.64 = bf16[2,16,16384]{2,1,0:T(8,128)(2,1)S(1)} custom-call(s32[2,2]{1,0:T(2,128)} %refs_0_.1, s32[16]{0:T(128)} %refs_1_.1, s32[256]{0:T(256)} %refs_2_.1, bf16[16,2,512]{2,1,0:T(2,128)(2,1)} %refs_3_.1, bf16[2,2,16896]{2,1,0:T(2,128)(2,1)} %bitcast.6, bf16[2,2,8704]{2,1,0:T(2,128)(2,1)} %bitcast.7), custom_call_target="tpu_custom_call" | custom-call | flops 4026531840 | bytes 1048576 | tf_op jit(solution)/shard_map/pallas_call | solution.py:461
  27.7 1.0 %copy.9 = bf16[2,1,16,16384]{3,2,1,0:T(8,128)(2,1)} copy(bf16[2,1,16,16384]{3,2,1,0:T(8,128)(2,1)S(1)} %bitcast.5) | data formatting | bytes 2097152

commit v7 on v6

--- a/solution.py
+++ b/solution.py
@@ -105,9 +105,12 @@
 
     def lay_out(self, held):
         for window in range(self.windows):
-            for number in range(self.channel_rows):
+
+
+            @pl.loop(0, self.channel_rows, unroll=4)
+            def _(number):
                 rows = pl.ds(window * self.window_rows + number, 2, stride=self.channel_rows)
-                lanes = pl.ds(number * LANES, LANES)
+                lanes = pl.ds(pl.multiple_of(number * LANES, LANES), LANES)
                 self.widened[rows, :] = held[window, :, lanes].astype(jnp.float32)
         rest = self.padded - self.rows
         if rest:
@@ -423,9 +426,12 @@
             totals[rows, :] = jnp.where(live > slot, total, 0.0)
 
     for window in range(windows):
-        for block in range(whole_blocks):
+
+        @pl.loop(0, whole_blocks, unroll=8)
+        def _(block):
             rows = pl.ds((window * whole_blocks + block) * pitch, per)
-            out_ref[window, :, pl.ds(block * LANES, LANES)] = totals[rows, :].astype(jnp.bfloat16)
+            lanes = pl.ds(pl.multiple_of(block * LANES, LANES), LANES)
+            out_ref[window, :, lanes] = totals[rows, :].astype(jnp.bfloat16)
 
     @pl.loop(1, width)
     def _(step):

time: 29.1 us -> 29.4 us (1.010)
  Pallas kernels: 27.7 us -> 28 us
where the time goes in v7:
time: 29.4 us; the launch traced here: 28.9 us
  Pallas kernels  28 us (95%)
  local copies, waits for them, and re-layouts  0.97 us (3%)
    pallas_call x1, Pallas kernels, body(): pl.pallas_call(functools.partial(kernel, plan), out_shape=jax.ShapeDtypeS...  28 us
    unnamed x1, local copies, waits for them, and re-layouts  0.97 us

profile of v7, /device:TPU:0, one launch (start us, length us, event | category | flops | bytes accessed | tf_op | source)
XLA Modules:
  0.0 28.9 jit_solution(16368676095611387103)
XLA Ops:
  0.0 28.0 %shard_map.64 = bf16[2,16,16384]{2,1,0:T(8,128)(2,1)S(1)} custom-call(s32[2,2]{1,0:T(2,128)} %refs_0_.1, s32[16]{0:T(128)} %refs_1_.1, s32[256]{0:T(256)} %refs_2_.1, bf16[16,2,512]{2,1,0:T(2,128)(2,1)} %refs_3_.1, bf16[2,2,16896]{2,1,0:T(2,128)(2,1)} %bitcast.6, bf16[2,2,8704]{2,1,0:T(2,128)(2,1)} %bitcast.7), custom_call_target="tpu_custom_call" | custom-call | flops 4026531840 | bytes 1048576 | tf_op jit(solution)/shard_map/pallas_call | solution.py:467
  28.0 1.0 %copy.9 = bf16[2,1,16,16384]{3,2,1,0:T(8,128)(2,1)} copy(bf16[2,1,16,16384]{3,2,1,0:T(8,128)(2,1)S(1)} %bitcast.5) | data formatting | bytes 2097152

commit v8 on v6

--- a/solution.py
+++ b/solution.py
@@ -413,7 +413,7 @@
     pitch = per + 1
     live = jnp.full((whole_blocks, LANES), counts_ref[column], jnp.int32)
 
-    @pl.loop(0, per, unroll=2)
+    @pl.loop(0, per, unroll=4)
     def _(slot):
         values = powers_of(whole.blocked, own_toeplitz[slot], whole_blocks)
         for window in range(windows):

time: 29.1 us -> 28.4 us (0.976)
  Pallas kernels: 27.7 us -> 27 us
    pallas_call x1, Pallas kernels: 27.7 us -> 27 us  [body(): pl.pallas_call(functools.partial(kernel, plan), out_shape=jax.ShapeDtypeS...]
where the time goes in v8:
time: 28.4 us; the launch traced here: 28 us
  Pallas kernels  27 us (95%)
  local copies, waits for them, and re-layouts  0.97 us (3%)
    pallas_call x1, Pallas kernels, body(): pl.pallas_call(functools.partial(kernel, plan), out_shape=jax.ShapeDtypeS...  27 us
    unnamed x1, local copies, waits for them, and re-layouts  0.97 us

profile of v8, /device:TPU:0, one launch (start us, length us, event | category | flops | bytes accessed | tf_op | source)
XLA Modules:
  0.0 28.0 jit_solution(7081920344710962959)
XLA Ops:
  0.0 27.0 %shard_map.64 = bf16[2,16,16384]{2,1,0:T(8,128)(2,1)S(1)} custom-call(s32[2,2]{1,0:T(2,128)} %refs_0_.1, s32[16]{0:T(128)} %refs_1_.1, s32[256]{0:T(256)} %refs_2_.1, bf16[16,2,512]{2,1,0:T(2,128)(2,1)} %refs_3_.1, bf16[2,2,16896]{2,1,0:T(2,128)(2,1)} %bitcast.6, bf16[2,2,8704]{2,1,0:T(2,128)(2,1)} %bitcast.7), custom_call_target="tpu_custom_call" | custom-call | flops 4026531840 | bytes 1048576 | tf_op jit(solution)/shard_map/pallas_call | solution.py:461
  27.0 1.0 %copy.9 = bf16[2,1,16,16384]{3,2,1,0:T(8,128)(2,1)} copy(bf16[2,1,16,16384]{3,2,1,0:T(8,128)(2,1)S(1)} %bitcast.5) | data formatting | bytes 2097152

commit v9 on v8

--- a/solution.py
+++ b/solution.py
@@ -389,7 +389,7 @@
 
     half.collect(chunks)
 
-    @pl.loop(0, per, unroll=4)
+    @pl.loop(0, per, unroll=8)
     def _(slot):
         values = powers_of(half.blocked, partner_toeplitz[slot], half_blocks)
         planes[slot] = jnp.concatenate(values, axis=0).astype(jnp.bfloat16)
@@ -398,7 +398,7 @@
     doubling_lane = lax.broadcasted_iota(jnp.int32, (LANES, 2 * LANES), 1)
     doubling = (doubling_row == doubling_lane // 2).astype(jnp.bfloat16)
 
-    @pl.loop(0, per, unroll=4)
+    @pl.loop(0, per, unroll=8)
     def _(slot):
         doubled = jnp.dot(planes[slot], doubling, preferred_element_type=jnp.float32)
         for window in range(windows):
@@ -413,7 +413,7 @@
     pitch = per + 1
     live = jnp.full((whole_blocks, LANES), counts_ref[column], jnp.int32)
 
-    @pl.loop(0, per, unroll=4)
+    @pl.loop(0, per, unroll=8)
     def _(slot):
         values = powers_of(whole.blocked, own_toeplitz[slot], whole_blocks)
         for window in range(windows):

time: 28.4 us -> 27.5 us (0.968)
  Pallas kernels: 27 us -> 26 us
    pallas_call x1, Pallas kernels: 27 us -> 26 us  [body(): pl.pallas_call(functools.partial(kernel, plan), out_shape=jax.ShapeDtypeS...]
where the time goes in v9:
time: 27.5 us; the launch traced here: 27 us
  Pallas kernels  26 us (95%)
  local copies, waits for them, and re-layouts  0.97 us (4%)
    pallas_call x1, Pallas kernels, body(): pl.pallas_call(functools.partial(kernel, plan), out_shape=jax.ShapeDtypeS...  26 us
    unnamed x1, local copies, waits for them, and re-layouts  0.97 us

profile of v9, /device:TPU:0, one launch (start us, length us, event | category | flops | bytes accessed | tf_op | source)
XLA Modules:
  0.0 27.0 jit_solution(12046308816995738395)
XLA Ops:
  0.0 26.0 %shard_map.64 = bf16[2,16,16384]{2,1,0:T(8,128)(2,1)S(1)} custom-call(s32[2,2]{1,0:T(2,128)} %refs_0_.1, s32[16]{0:T(128)} %refs_1_.1, s32[256]{0:T(256)} %refs_2_.1, bf16[16,2,512]{2,1,0:T(2,128)(2,1)} %refs_3_.1, bf16[2,2,16896]{2,1,0:T(2,128)(2,1)} %bitcast.6, bf16[2,2,8704]{2,1,0:T(2,128)(2,1)} %bitcast.7), custom_call_target="tpu_custom_call" | custom-call | flops 4026531840 | bytes 1048576 | tf_op jit(solution)/shard_map/pallas_call | solution.py:461
  26.0 1.0 %copy.9 = bf16[2,1,16,16384]{3,2,1,0:T(8,128)(2,1)} copy(bf16[2,1,16,16384]{3,2,1,0:T(8,128)(2,1)S(1)} %bitcast.5) | data formatting | bytes 2097152
